TPU v7x, 128 devices: a whole 4x4x4 slice. The times are simulated.
128 devices in a mesh: scene: 32 (over x, z, core), tie: 4 (over y).
Axes of the slice: x: 4, y: 4, z: 4, core: 2. Of those that a mesh axis runs over, the one named last changes fastest.
Arguments:
- tie_rows: bfloat16 [384, 256, 256], P('tie'), may hold values from -0.375 to 0.375
- point_counts: int32 [384], P('tie'), may hold values from 1 to 128, as said below
- pattern: int32 [512, 384], P('scene', 'tie'), may hold values 0 or 1
- sensitivity: bfloat16 [512, 192, 192], P('scene'), may hold values from -0.119628906 to 0.119628906
- damping: float32 [512], P(('scene', 'tie')), may hold values from 1 to 8
- prior: float32 [64], replicated, may hold values from 0.25 to 4
Outputs:
- scene_rows: float32 [512, 192, 256], P(('scene', 'tie'))
- global_factor: float32 [64, 64], replicated
Inputs may be any that keep to these rules, and one draw needn't show every extreme that they name: `point_counts`: points present in each block; some block is full.
All inputs are finite; a program needn't handle non-finite values. No bound on the sum of `pattern` on one device may be relied on, other than what follows from the above.
Results may differ from a plain program's by a relative error of at most 0.0003.
Values sent between devices are 32-bit elements; how exact they have to be, the bound alone decides.
No kernel may reach another device: no remote copies, remote signals or barrier semaphores. Data moves between devices by JAX's collectives and lax.ppermute only.
A program may use at most 128 MiB of HBM per device.

v0:
```python
import jax
import jax.numpy as jnp
from jax import lax
from jax.sharding import PartitionSpec as P

SPLINE = 192


highest = lax.Precision.HIGHEST


def merged_2(value, axis, join):
    pieces = lax.all_gather(value, axis)
    head = pieces[0]
    tail = pieces[1:]
    running, _ = lax.scan(lambda running, share: (join(running, share), None), head, tail)
    return running


def block_gram(tie_rows, point_counts):
    row_index = lax.broadcasted_iota(jnp.int32, (tie_rows.shape[0], tie_rows.shape[1]), 1)
    row_valid = (row_index // 2 < point_counts[:, None]).astype(tie_rows.dtype)
    masked_rows = tie_rows * row_valid[:, :, None]
    return lax.dot_general(
        masked_rows, tie_rows, (((1,), (1,)), ((0,), (0,))), preferred_element_type=jnp.float32
    )


def scene_info(merged, sensitivity, width):
    basis = jnp.eye(width, dtype=jnp.float32)[None] + sensitivity.astype(jnp.float32)
    corner = merged[:, :width, :width]
    side = merged[:, :width, width:]
    tail = merged[:, width:, width:]
    mixed = jnp.einsum("sab,sbc->sac", corner, basis, precision=highest)
    corner_new = jnp.einsum("sba,sbc->sac", basis, mixed, precision=highest)
    side_new = jnp.einsum("sba,sbc->sac", basis, side, precision=highest)
    upper_half = jnp.concatenate([corner_new, side_new], 2)
    lower_half = jnp.concatenate([jnp.transpose(side_new, (0, 2, 1)), tail], 2)
    return jnp.concatenate([upper_half, lower_half], 1)


def factor_scenes(information, damping, width):
    total_width = information.shape[1]
    column_index = lax.broadcasted_iota(jnp.int32, (information.shape[0], total_width), 1)
    added = jnp.where(column_index < width, damping[:, None], 1.0)
    shifted = information + added[:, :, None] * jnp.eye(total_width, dtype=jnp.float32)[None]
    whole_lower = jnp.linalg.cholesky(shifted)
    chol_lower = whole_lower[:, :width, :width]
    cross = jnp.transpose(whole_lower[:, width:, :width], (0, 2, 1))
    tail_lower = whole_lower[:, width:, width:]
    shared_eye = jnp.eye(total_width - width, dtype=jnp.float32)
    reduced = (
        jnp.einsum("sab,scb->sac", tail_lower, tail_lower, precision=highest) - shared_eye[None]
    )
    out_rows = jnp.concatenate([jnp.transpose(chol_lower, (0, 2, 1)), cross], 2)
    return (out_rows, jnp.sum(reduced, 0))


def unite(first, second):
    gram_sum = jnp.dot(first.T, first, precision=highest) + jnp.dot(
        second.T, second, precision=highest
    )
    return jnp.transpose(jnp.linalg.cholesky(gram_sum))


def on_device(tie_rows, point_counts, pattern, sensitivity, damping, prior):
    block_grams = block_gram(tie_rows, point_counts)
    width = block_grams.shape[1]
    grams_flat = block_grams.reshape(block_grams.shape[0], width * width)
    merged = jnp.dot(pattern.astype(jnp.float32), grams_flat, precision=highest).reshape(
        pattern.shape[0], width, width
    )
    payload = scene_info(merged, sensitivity, SPLINE)
    summed = lax.psum_scatter(payload, "tie", scatter_dimension=0, tiled=True)
    owned = damping.shape[0]
    scene_rows, reduced = factor_scenes(summed, damping, SPLINE)
    devices = lax.axis_size("scene") * lax.axis_size("tie")
    local_info = reduced / (owned * devices) + jnp.diag(prior) / devices
    local_factor = jnp.transpose(jnp.linalg.cholesky(local_info))
    global_factor = merged_2(local_factor, ("scene", "tie"), unite)
    return (scene_rows, global_factor)


def solution(mesh):
    placed = (
        P("tie", None, None),
        P("tie"),
        P("scene", "tie"),
        P("scene", None, None),
        P(("scene", "tie")),
        P(),
    )
    return jax.shard_map(
        on_device,
        mesh=mesh,
        in_specs=placed,
        out_specs=(P(("scene", "tie"), None, None), P()),
        check_vma=False,
    )
```

profile of v0, /device:TPU:0, one launch (start us, length us, event | category | flops | bytes accessed | tf_op | source)
XLA Modules:
  0.0 1466.2 jit_solution(2726832421665589131)
XLA Ops:
  8.0 23.1 %fusion.4 = f32[96,256,256]{2,1,0:T(8,128)} fusion(bf16[96,256,256]{2,1,0:T(8,128)(2,1)} %param.9, bf16[96,256]{1,0:T(8,128)(2,1)S(1)} %fusion.23), kind=kOutput, calls=%fused_computation.11 | convolution fusion | flops 3227516928 | bytes 37797888 | tf_op jit(solution)/shard_map/dot_general | solution.py:24
  31.1 21.7 %copy.91 = f32[12,8,256,256]{3,1,2,0:T(8,128)S(1)} copy(f32[12,8,256,256]{3,2,1,0:T(8,128)} %bitcast.57) | data formatting | bytes 50331648
  52.8 13.7 fusion.26
  77.0 16.6 %fusion.10 = f32[16,192,192]{1,2,0:T(8,128)S(1)} fusion(f32[16,192,192]{2,1,0:T(8,128)S(1)} %fusion.7, bf16[16,192,192]{2,1,0:T(8,128)(2,1)S(1)} %copy-done, f32[192,192]{1,0:T(8,128)S(1)} %fusion.21), kind=kOutput, calls=%fused_computation.19 | convolution fusion | flops 1360134144 | bytes 6045696 | tf_op jit(solution)/shard_map/sba,sbc->sac/dot_general | solution.py:35
  103.9 48.8 %reduce-scatter.2.cloned.1.call-done = f32[4,256,256]{1,2,0:T(8,128)} async-done(((f32[16,256,256]{1,2,0:T(8,128)}), f32[4,256,256]{1,2,0:T(8,128)}) %reduce-scatter.2.cloned.1.call-update) | async-done | bytes 1048592 | tf_op jit(solution)/shard_map/reduce_scatter | solution.py:74
  154.6 46.9 %custom-call.15 = f32[4,128,128]{2,1,0:T(8,128)S(1)} custom-call(f32[4,128,128]{2,1,0:T(8,128)S(1)} %cholesky.186), custom_call_target="Cholesky" | custom-call | tf_op jit(solution)/shard_map/jit(cholesky)/cholesky | solution.py:47
  201.7 39.3 %custom-call.16 = f32[4,1,128,128]{2,3,1,0:T(8,128)S(1)} custom-call(f32[4,1,128,128]{3,2,1,0:T(8,128)S(1)} %select_bitcast_fusion.1), custom_call_target="InvertDiagBlocksLowerTriangular" | custom-call | tf_op jit(solution)/shard_map/jit(cholesky)/cholesky | solution.py:47
  242.1 47.1 %custom-call.17 = f32[4,128,128]{2,1,0:T(8,128)S(1)} custom-call(f32[4,128,128]{2,1,0:T(8,128)S(1)} %convolution_subtract_fusion), custom_call_target="Cholesky" | custom-call | tf_op jit(solution)/shard_map/jit(cholesky)/cholesky | solution.py:47
  299.6 65.4 %all-gather.3.cloned.1.call-done = f32[8192,64]{1,0:T(8,128)} async-done(((f32[64,64]{1,0:T(8,128)}), f32[8192,64]{1,0:T(8,128)}) %all-gather.3.cloned.1.call-update) | async-done | bytes 2097168 | tf_op jit(solution)/shard_map/all_gather | solution.py:13
  370.2 1088.2 %while.10 = (s32[]{:T(128)}, f32[64,64]{0,1:T(8,128)S(1)}, f32[127,64,64]{2,1,0:T(8,128)}, s32[]{:T(128)}) while((s32[]{:T(128)}, f32[64,64]{0,1:T(8,128)S(1)}, f32[127,64,64]{2,1,0:T(8,128)}, s32[]{:T(128)}) %tuple.42), condition=%wide.region_9.11_spmd, body=%wide.region_8.10_spmd.sunk | while | flops 6328385 | bytes 230455 | solution.py:16
  380.2 5.8 cholesky.275
  388.7 5.8 cholesky.275
  397.3 5.8 cholesky.275
  405.9 5.8 cholesky.275
  414.4 5.8 cholesky.275
  423.0 5.8 cholesky.275
  431.6 5.8 cholesky.275
  440.1 5.8 cholesky.275
  465.8 5.8 cholesky.275
  474.4 5.8 cholesky.275
  483.0 5.8 cholesky.275
  491.5 5.8 cholesky.275
  508.7 5.8 cholesky.275
  517.3 5.8 cholesky.275
  525.8 5.8 cholesky.275
  534.4 5.8 cholesky.275
  551.5 5.8 cholesky.275
  560.1 5.8 cholesky.275
  577.2 5.8 cholesky.275
  602.9 5.8 cholesky.275
  611.5 5.8 cholesky.275
  620.1 5.8 cholesky.275
  628.6 5.8 cholesky.275
  637.2 5.8 cholesky.275
  645.8 5.8 cholesky.275
  654.4 5.8 cholesky.275
  671.5 5.8 cholesky.275
  697.2 5.8 cholesky.275
  705.8 5.8 cholesky.275
  731.5 5.8 cholesky.275
  740.0 5.8 cholesky.275
  748.6 5.8 cholesky.275
  765.7 5.8 cholesky.275
  774.3 5.8 cholesky.275
  782.9 5.8 cholesky.275
  791.5 5.8 cholesky.275
  800.0 5.8 cholesky.275
  825.7 5.8 cholesky.275
  834.3 5.8 cholesky.275
  842.9 5.8 cholesky.275
  851.4 5.8 cholesky.275
  868.6 5.8 cholesky.275
  877.1 5.8 cholesky.275
  885.7 5.8 cholesky.275
  894.3 5.8 cholesky.275
  911.4 5.8 cholesky.275
  920.0 5.8 cholesky.275
  928.6 5.8 cholesky.275
  945.7 5.8 cholesky.275
  962.8 5.8 cholesky.275
  971.4 5.8 cholesky.275
  980.0 5.8 cholesky.275
  988.5 5.8 cholesky.275
  997.1 5.8 cholesky.275
  (1026 shorter events, 806.4 us)
Async XLA Ops:
  7.2 145.5 %reduce-scatter.2.cloned.1.call-start = ((), (), s32[]{:S(2)}) async-start(), calls=%async_computation.1 | async-start | bytes 5242880 | tf_op jit(solution)/shard_map/reduce_scatter | solution.py:74
  31.1 21.7 %copy-start.2 = (s32[16,96]{1,0:T(8,128)S(1)}, s32[16,96]{1,0:T(8,128)}, u32[]{:S(2)}) copy-start(s32[16,96]{1,0:T(8,128)} %param.11) | copy-start | bytes 18436
  66.5 1.4 copy-start
  103.2 0.7 copy-start.4
  103.2 261.8 %all-gather.3.cloned.1.call-start = ((), (), s32[]{:S(2)}) async-start(), calls=%async_computation.2 | async-start | bytes 4227072 | tf_op jit(solution)/shard_map/all_gather | solution.py:13
  152.7 1.8 copy-start.1
  154.6 135.5 %copy-start.3 = (f32[64]{0:T(128)S(1)}, f32[64]{0:T(128)}, u32[]{:S(2)}) copy-start(f32[64]{0:T(128)} %param.14) | copy-start | bytes 772
Sparse Core Ops, SparseCore 0:
  103.3 49.2 reduce-scatter.1
  298.3 66.6 all-gather.2
where the time goes:
time: 1480 us; the launch traced here: 1470 us
  other arithmetic  1060 us (72%)
  matrix products  223 us (15%)
  waiting for transfers between devices  114 us (8%)
  local copies, waits for them, and re-layouts  47.5 us (3%)
    another operation x381, other arithmetic, unite(): return jnp.transpose(jnp.linalg.cholesky(gram_sum))  828 us
    dot_general x127, matrix products, unite(): jnp.dot(second.T, second, precision=highest)  136 us
    another operation x10, other arithmetic, factor_scenes(): whole_lower = jnp.linalg.cholesky(shifted)  134 us
    transpose x127, other arithmetic, unite(): return jnp.transpose(jnp.linalg.cholesky(gram_sum))  82.8 us
    all_gather x1, waiting for transfers between devices, merged_2(): pieces = lax.all_gather(value, axis)  65.4 us
    reduce_scatter x1, waiting for transfers between devices, on_device(): summed = lax.psum_scatter(payload, 'tie', scatter_dimension=0, tiled=True)  48.8 us
  transfers between devices with their start and end apart: 2, of which 2 were waited for; matrix products, arithmetic and copies ran while one was open for 0% of the time, Pallas kernels for 0%

commit v1 on v0

v1 whole, which is shorter than its diff:
```python
import functools

import jax
import jax.numpy as jnp
from jax import lax
from jax.experimental import pallas as pl
from jax.experimental.pallas import tpu as pltpu
from jax.sharding import PartitionSpec as P

SPLINE = 192
SHARED = 64
COLS = 256
PACK = 264
PANEL = 32
N_PANEL = SPLINE // PANEL
UNROLL = 4
DEPTH = 16
f32 = jnp.float32
bf16 = jnp.bfloat16


def iota(shape, axis):
    return lax.broadcasted_iota(jnp.int32, shape, axis)


def split(x):
    high = x.astype(bf16)
    return high, (x - high.astype(f32)).astype(bf16)


def dot(a, b, contract=((1,), (0,))):
    return lax.dot_general(a, b, (contract, ((), ())), preferred_element_type=f32)


def dot3(a, b, contract=((1,), (0,))):
    a_high, a_low = split(a)
    b_high, b_low = split(b)
    return dot(a_high, b_high, contract) + (dot(a_low, b_high, contract) + dot(a_high, b_low, contract))


def outer_panel(left_high, left_low, right_high, right_low):
    left = jnp.concatenate([left_high, left_low, left_high, left_low], 0)
    right = jnp.concatenate([right_high, right_high, right_low, right_low], 0)
    return dot(left, right, ((0,), (0,)))


def invert_lower(packed):
    lane = iota((PANEL, 128), 1)
    group = lane - lax.rem(lane, PANEL)
    blocks = PANEL // 8
    sub = iota((8, 128), 0)
    columns = []
    for j in range(PANEL):
        wide = jnp.take_along_axis(packed, group + j, axis=1)
        columns.append([wide[8 * v:8 * v + 8] for v in range(blocks)])
    ident = (iota((PANEL, 128), 0) == lax.rem(lane, PANEL)).astype(f32)
    x = [ident[8 * v:8 * v + 8] for v in range(blocks)]

    def spread(block, at):
        return jnp.broadcast_to(block[at:at + 1], (8, 128))

    for k in range(PANEL):
        kv, ks = divmod(k, 8)
        scale = lax.rsqrt(spread(columns[k][kv], ks))
        lower = [None] * blocks
        for v in range(kv, blocks):
            lower[v] = columns[k][v] * scale
        for j in range(k + 1, PANEL):
            jv, js = divmod(j, 8)
            factor = spread(lower[jv], js)
            for v in range(jv, blocks):
                columns[j][v] = columns[j][v] - lower[v] * factor
        row = spread(x[kv], ks) * scale
        for v in range(kv, blocks):
            if v == kv:
                below = jnp.where(sub > ks, lower[v], 0.0)
                x[v] = jnp.where(sub == ks, row, x[v] - below * row)
            else:
                x[v] = x[v] - lower[v] * row
    return jnp.concatenate(x, 0)


def factor_kernel(damp_ref, own_ref, below_refs, above_refs, sens_ref, rows_ref, sum_ref, work):
    owned = rows_ref.shape[0]
    r1, c1 = iota((128, 128), 0), iota((128, 128), 1)
    tail_sum = jnp.zeros((SHARED, 128), f32)
    for s in range(owned):
        arrived, at = (below_refs, s) if s < owned // 2 else (above_refs, s - owned // 2)
        part = own_ref[s] + (arrived[0][at] + arrived[1][at])
        packed, side = part[:128], part[128:256]
        diagonal = jnp.sum(part[256:264], axis=0, keepdims=True)
        turned = packed.T
        first = jnp.where(r1 <= c1, packed, turned)
        last = jnp.where(r1 > c1, packed, jnp.where(r1 == c1, diagonal, turned))
        tail_sum = tail_sum + last[SHARED:]
        top = jnp.concatenate([
            jnp.concatenate([first, side], 1),
            jnp.concatenate([side.T[:SPLINE - 128], last[:SPLINE - 128]], 1),
        ], 0)
        sens = sens_ref[s]
        wide_sens = jnp.concatenate([sens, jnp.zeros((SPLINE, SHARED), bf16)], 1)
        high, low = split(top[:, :SPLINE])
        mixed = top + dot(high, wide_sens) + dot(low, wide_sens)
        high, low = split(mixed)
        both = ((0,), (0,))
        square = jnp.concatenate([wide_sens, jnp.zeros((COLS - SPLINE, COLS), bf16)], 0)
        pad = jnp.zeros((COLS - SPLINE, COLS), bf16)
        high, low = jnp.concatenate([high, pad], 0), jnp.concatenate([low, pad], 0)
        info = mixed + (dot(square, high, both) + dot(square, low, both))[:SPLINE]
        info = info + jnp.where(iota((SPLINE, COLS), 0) == iota((SPLINE, COLS), 1), damp_ref[s], 0.0)
        for p in range(N_PANEL):
            work[p, s * PANEL:(s + 1) * PANEL] = info[p * PANEL:(p + 1) * PANEL]
    tail_sum = tail_sum[:, SHARED:]

    lane = iota((PANEL, 128), 1)
    same = (r1 // PANEL) == (c1 // PANEL)
    row_in = lax.rem(iota((128, COLS), 0), PANEL)
    col_in = iota((128, COLS), 1)
    for p in range(N_PANEL):
        half, inner = divmod(p * PANEL, 128)
        current = work[p]
        packed = jnp.zeros((PANEL, 128), f32)
        for s in range(owned):
            piece = current[s * PANEL:(s + 1) * PANEL, half * 128:(half + 1) * 128]
            shift = (s * PANEL - inner) % 128
            if shift:
                piece = pltpu.roll(piece, shift, 1)
            packed = jnp.where(lane // PANEL == s, piece, packed)
        inverse = invert_lower(packed)
        spread = jnp.where(same, jnp.concatenate([inverse] * (128 // PANEL), 0), 0.0)
        rows = dot3(spread, current)
        rows = jnp.where(col_in >= row_in + p * PANEL, rows, 0.0)
        for s in range(owned):
            rows_ref[s, p * PANEL:(p + 1) * PANEL] = rows[s * PANEL:(s + 1) * PANEL]
        high, low = split(rows)
        start = ((p + 1) * PANEL) // 128 * 128
        if p + 1 < N_PANEL:
            for s in range(owned):
                at = slice(s * PANEL, (s + 1) * PANEL)
                update = outer_panel(high[at, start:], low[at, start:], high[at], low[at])
                for q in range(p + 1, N_PANEL):
                    work[q, at] = work[q, at] - update[q * PANEL - start:(q + 1) * PANEL - start]
        cross_high, cross_low = high[:, 128:], low[:, 128:]
        both = ((0,), (0,))
        outer = dot(cross_high, cross_high, both) + (dot(cross_high, cross_low, both) + dot(cross_low, cross_high, both))
        tail_sum = tail_sum - outer[SHARED:, SHARED:]
    sum_ref[...] = tail_sum


def factor_scenes(own, below, above, sens, damping):
    owned = damping.shape[0]
    vmem = pl.BlockSpec(memory_space=pltpu.VMEM)

    def kernel(damp_ref, own_ref, b0, b1, a0, a1, *rest):
        factor_kernel(damp_ref, own_ref, (b0, b1), (a0, a1), *rest)

    return pl.pallas_call(
        kernel,
        out_shape=(
            jax.ShapeDtypeStruct((owned, SPLINE, COLS), f32),
            jax.ShapeDtypeStruct((SHARED, SHARED), f32),
        ),
        in_specs=[pl.BlockSpec(memory_space=pltpu.SMEM)] + [vmem] * 6,
        out_specs=(vmem, vmem),
        scratch_shapes=[pltpu.VMEM((N_PANEL, owned * PANEL, COLS), f32)],
        compiler_params=pltpu.CompilerParams(vmem_limit_bytes=32 * 1024 * 1024),
        name="factor_scenes",
    )(damping, own, *below, *above, sens)


def total_kernel(n_parts, count, *refs):
    prior_ref = refs[0]
    out_ref = refs[-1]
    total = refs[1][...]
    for other in refs[2:-1]:
        total = total + other[...]
    total = total / count
    r, c = iota((SHARED, SHARED), 0), iota((SHARED, SHARED), 1)
    total = total + jnp.where(r == c, prior_ref[...], 0.0)
    pad = jnp.zeros((SHARED, 128 - SHARED), f32)
    wide = jnp.concatenate([total, pad], 1)
    top, bottom = wide[:PANEL], wide[PANEL:]
    lane = iota((PANEL, 128), 1)
    row = iota((PANEL, 128), 0)
    inverse = invert_lower(top)
    upper = dot3(jnp.where(lane < PANEL, inverse, 0.0)[:, :PANEL], top)
    upper = jnp.where(lane >= row, upper, 0.0)
    high, low = split(upper)
    bottom = bottom - outer_panel(high, low, high, low)[PANEL:SHARED]
    moved = pltpu.roll(bottom, 128 - PANEL, 1)
    inverse = invert_lower(moved)
    lower = dot3(inverse[:, :PANEL], bottom)
    lower = jnp.where(lane >= row + PANEL, lower, 0.0)
    out_ref[...] = jnp.concatenate([upper[:, :SHARED], lower[:, :SHARED]], 0)


def factor_total(parts, prior, count):
    vmem = pl.BlockSpec(memory_space=pltpu.VMEM)
    return pl.pallas_call(
        functools.partial(total_kernel, len(parts), count),
        out_shape=jax.ShapeDtypeStruct((SHARED, SHARED), f32),
        in_specs=[vmem] * (1 + len(parts)),
        out_specs=vmem,
        name="factor_total",
    )(prior.reshape(1, SHARED), *parts)


def gram_kernel(groups, me_ref, pat_ref, cnt_ref, tie_ref, *rest):
    n_out = len(groups)
    outs = rest[:n_out]
    acc, held, pairs, sems = rest[n_out:]
    n_block = tie_ref.shape[0]
    slots = [(distance, scene) for distance, scenes in groups for scene in scenes]
    n_slot = len(slots)
    ways = 4
    found = jnp.int32(0)
    for slot, (distance, scene) in enumerate(slots):
        row = lax.rem(me_ref[0] + distance, ways) * (pat_ref.shape[0] // ways) + scene

        def some(i, found, slot=slot, row=row):
            for j in range(8):
                block = i * 8 + j
                pairs[found] = slot * 1024 + block
                found = found + pat_ref[row, block]
            return found

        found = lax.fori_loop(0, n_block // 8, some, found)
    for j in range(UNROLL):
        pairs[found + j] = n_slot * 1024
    rounds = lax.div(found + (UNROLL - 1), UNROLL)
    rings = DEPTH // UNROLL

    def fetch(index, slot):
        return pltpu.make_async_copy(
            tie_ref.at[lax.bitwise_and(pairs[index], 1023)], held.at[slot], sems.at[slot]
        )

    for g in range(rings):
        @pl.when(g < rounds)
        def _():
            for j in range(UNROLL):
                fetch(g * UNROLL + j, g * UNROLL + j).start()

    acc[...] = jnp.zeros_like(acc)
    row_at = iota((COLS, COLS), 0)
    r1, c1 = iota((128, 128), 0), iota((128, 128), 1)
    both = ((0,), (0,))

    def step(i, carry):
        base = lax.rem(i, rings) * UNROLL
        for j in range(UNROLL):
            fetch(i * UNROLL + j, base + j).wait()
        for j in range(UNROLL):
            pair = pairs[i * UNROLL + j]
            slot = lax.shift_right_logical(pair, 10)
            rows = held[base + j]
            kept = jnp.where(row_at < 2 * cnt_ref[lax.bitwise_and(pair, 1023)], rows, jnp.zeros_like(rows))
            top = dot(kept[:, :128], rows, both)
            last = dot(kept[:, 128:], rows[:, 128:], both)
            acc[slot, 0:128] += jnp.where(r1 <= c1, top[:, :128], last)
            acc[slot, 128:256] += top[:, 128:]
            acc[slot, 256:264] += jnp.sum(jnp.where(r1 == c1, last, 0.0).reshape(16, 8, 128), axis=0)

        @pl.when(i + rings < rounds)
        def _():
            for j in range(UNROLL):
                fetch((i + rings) * UNROLL + j, base + j).start()
        return carry

    lax.fori_loop(0, rounds, step, 0)
    at = 0
    for out, (distance, scenes) in zip(outs, groups):
        out[...] = acc[at:at + len(scenes)]
        at += len(scenes)


def partial_grams(me, pattern, counts, tie_rows, groups):
    smem = pl.BlockSpec(memory_space=pltpu.SMEM)
    vmem = pl.BlockSpec(memory_space=pltpu.VMEM)
    n_slot = sum(len(scenes) for _, scenes in groups)
    n_pairs = n_slot * tie_rows.shape[0] + UNROLL
    return pl.pallas_call(
        functools.partial(gram_kernel, groups),
        out_shape=[jax.ShapeDtypeStruct((len(scenes), PACK, 128), f32) for _, scenes in groups],
        in_specs=[smem, smem, smem, pl.BlockSpec(memory_space=pl.ANY)],
        out_specs=[vmem] * len(groups),
        scratch_shapes=[
            pltpu.VMEM((n_slot + 1, PACK, 128), f32),
            pltpu.VMEM((DEPTH, COLS, COLS), bf16),
            pltpu.SMEM(((n_pairs + 127) // 128 * 128,), jnp.int32),
            pltpu.SemaphoreType.DMA((DEPTH,)),
        ],
        compiler_params=pltpu.CompilerParams(vmem_limit_bytes=56 * 1024 * 1024),
        name="partial_grams",
    )(me, pattern, counts, tie_rows)


def ring(step, size):
    return [(i, (i + step) % size) for i in range(size)]


def swap(bits, size):
    return [(i, i ^ bits) for i in range(size)]


def on_device(tie_rows, point_counts, pattern, sensitivity, damping, prior):
    owned = damping.shape[0]
    ways = lax.axis_size("tie")
    me = lax.axis_index("tie")
    me_word = me.reshape(1).astype(jnp.int32)
    near, far = (0, 1), (2, 3)
    up = functools.partial(lax.ppermute, axis_name="tie", perm=ring(1, ways))
    down = functools.partial(lax.ppermute, axis_name="tie", perm=ring(-1, ways))

    far_up, far_down = partial_grams(me_word, pattern, point_counts, tie_rows, ((2, near), (2, far)))
    came_up, came_down = up(far_up), down(far_down)
    up_now, up_later, down_now, down_later, own = partial_grams(
        me_word, pattern, point_counts, tie_rows,
        ((1, far), (1, near), (3, near), (3, far), (0, near + far)),
    )
    sens = lax.dynamic_slice_in_dim(sensitivity, me * owned, owned, 0)
    got_up, got_down = up(up_now), down(down_now)
    last_up, last_down = up(up_later + came_up), down(down_later + came_down)
    scene_rows, reduced = factor_scenes(own, (last_up, got_down), (got_up, last_down), sens, damping)

    n_scene = lax.axis_size("scene")
    total = reduced
    for axis, bits in (("scene", 1), ("tie", 1), ("tie", 3), ("scene", 2), ("scene", 6), ("scene", 8)):
        total = total + lax.ppermute(total, axis, swap(bits, lax.axis_size(axis)))
    other = lax.ppermute(total, "scene", swap(24, n_scene))
    global_factor = factor_total((total, other), prior, float(owned * n_scene * ways))
    return (scene_rows, global_factor)


def solution(mesh):
    placed = (
        P("tie", None, None),
        P("tie"),
        P("scene", "tie"),
        P("scene", None, None),
        P(("scene", "tie")),
        P(),
    )
    return jax.shard_map(
        on_device,
        mesh=mesh,
        in_specs=placed,
        out_specs=(P(("scene", "tie"), None, None), P()),
        check_vma=False,
    )
```

time: 1480 us -> 84.7 us (0.06)
  other arithmetic: 1060 us -> 2.7 us
  matrix products: 223 us -> 0 us
  waiting for transfers between devices: 114 us -> 28.6 us
  local copies, waits for them, and re-layouts: 47.5 us -> 0.65 us
  Pallas kernels: 0 us -> 32.3 us
  starting transfers between devices: 0.08 us -> 19.2 us
    another operation x394 -> x0, other arithmetic: 968 us -> none  [the longest x381 828 us: unite(): return jnp.transpose(jnp.linalg.cholesky(gram_sum))]
    dot_general x260 -> x0, matrix products: 222 us -> none  [the longest x127 136 us: unite(): jnp.dot(second.T, second, precision=highest)]
    transpose x128 -> x0, other arithmetic: 83.4 us -> none  [the longest x127 82.8 us: unite(): return jnp.transpose(jnp.linalg.cholesky(gram_sum))]
    all_gather x1 -> x0, waiting for transfers between devices: 65.4 us -> none  [merged_2(): pieces = lax.all_gather(value, axis)]
    reduce_scatter x1 -> x0, waiting for transfers between devices: 48.8 us -> none  [on_device(): summed = lax.psum_scatter(payload, 'tie', scatter_dimension=0, tiled=True)]
    pallas_call x0 -> x4, Pallas kernels: none -> 32.3 us  [the longest x2 19.7 us: partial_grams(): pl.pallas_call(functools.partial(gram_kernel, groups), out_shape=[jax.Sha...]
    ppermute x0 -> x13, waiting for transfers between devices: none -> 28.6 us  [the longest x6 17.6 us: on_device(): total = total + lax.ppermute(total, axis, swap(bits, lax.axis_size(axis)))]
    unnamed x15 -> x10, local copies, waits for them, and re-layouts: 27.5 us -> 0.63 us
  transfers between devices with their start and end apart: 2 -> 13, of which waited for: 2 -> 10; matrix products, arithmetic and copies ran while one was open for 0% -> 3% of each run, Pallas kernels for 0% -> 15%
where the time goes in v1:
time: 84.7 us; the launch traced here: 84.2 us
  Pallas kernels  32.3 us (38%)
  waiting for transfers between devices  28.6 us (34%)
  starting transfers between devices  19.2 us (23%)
  other arithmetic  2.7 us (3%)
    pallas_call x2, Pallas kernels, partial_grams(): pl.pallas_call(functools.partial(gram_kernel, groups), out_shape=[jax.Sha...  19.7 us
    ppermute x6, waiting for transfers between devices, on_device(): total = total + lax.ppermute(total, axis, swap(bits, lax.axis_size(axis)))  17.6 us
    pallas_call x1, Pallas kernels, factor_scenes(): pl.pallas_call(kernel, out_shape=(jax.ShapeDtypeStruct((owned, SPLINE, CO...  9.46 us
    ppermute x6, starting transfers between devices, on_device(): total = total + lax.ppermute(total, axis, swap(bits, lax.axis_size(axis)))  6.75 us
    ppermute x2, waiting for transfers between devices, on_device(): got_up, got_down = (up(up_now), down(down_now))  4.8 us
    ppermute x2, waiting for transfers between devices, on_device(): last_up, last_down = (up(up_later + came_up), down(down_later + came_down))  3.4 us
    ppermute x2, starting transfers between devices, on_device(): got_up, got_down = (up(up_now), down(down_now))  3.39 us
    ppermute x2, starting transfers between devices, on_device(): last_up, last_down = (up(up_later + came_up), down(down_later + came_down))  3.31 us
  transfers between devices with their start and end apart: 13, of which 10 were waited for; matrix products, arithmetic and copies ran while one was open for 3% of the time, Pallas kernels for 15%

profile of v1, /device:TPU:0, one launch (start us, length us, event | category | flops | bytes accessed | tf_op | source)
XLA Modules:
  0.0 84.2 jit_solution(10270877942854289852)
XLA Ops:
  0.6 0.0 copy-start
  0.6 6.8 %partial_grams.3 = (f32[2,264,128]{2,1,0:T(8,128)}, f32[2,264,128]{2,1,0:T(8,128)}) custom-call(s32[1]{0:T(128)} %bitcast.me_ref, s32[16,96]{1,0:T(8,128)} %pat_ref.3, s32[96]{0:T(128)} %cnt_ref.3, bf16[96,256,256]{2,1,0:T(8,128)(2,1)} %tie_ref.3), custom_call_target="tpu_custom_call" | custom-call | tf_op jit(solution)/shard_map/partial_grams/pallas_call | solution.py:282
  7.4 1.0 %collective-permute-start = (f32[2,264,128]{2,1,0:T(8,128)}, f32[2,264,128]{2,1,0:T(8,128)S(1)}, u32[]{:S(2)}, u32[]{:S(2)}) collective-permute-start(f32[2,264,128]{2,1,0:T(8,128)} %get-tuple-element.13), channel_id=1, source_target_pairs={{0,1},{1,2},{2,3},{3,0},{4,5},{5,6},{6,7},{7,4},{8,9},{9,10},{10,1... | collective-permute-start | bytes 811016 | tf_op jit(solution)/shard_map/ppermute | solution.py:316
  8.5 2.3 %collective-permute-start.4 = (f32[2,264,128]{2,1,0:T(8,128)}, f32[2,264,128]{2,1,0:T(8,128)S(1)}, u32[]{:S(2)}, u32[]{:S(2)}) collective-permute-start(f32[2,264,128]{2,1,0:T(8,128)} %get-tuple-element.17), channel_id=1, source_target_pairs={{0,3},{1,0},{2,1},{3,2},{4,7},{5,4},{6,5},{7,6},{8,11},{9,8},{10,9... | collective-permute-start | bytes 811016 | tf_op jit(solution)/shard_map/ppermute | solution.py:316
  10.7 12.9 %partial_grams.2 = (f32[2,264,128]{2,1,0:T(8,128)}, f32[2,264,128]{2,1,0:T(8,128)}, f32[2,264,128]{2,1,0:T(8,128)}, f32[2,264,128]{2,1,0:T(8,128)}, f32[4,264,128]{2,1,0:T(8,128)}) custom-call(s32[1]{0:T(128)} %bitcast.me_ref, s32[16,96]{1,0:T(8,128)} %pat_ref.3, s32[96]{0:T(128)} %cnt_ref.3, bf16[96,256,256]{2,1,0:T(8,128)(2,1)} %tie_ref.3), custom_call_target="tpu_custom_call" | custom-call | tf_op jit(solution)/shard_map/partial_grams/pallas_call | solution.py:282
  23.6 0.0 copy-start.1
  23.6 0.0 copy-start.2
  23.7 3.4 %collective-permute-start.2 = (f32[2,264,128]{2,1,0:T(8,128)}, f32[2,264,128]{2,1,0:T(8,128)S(1)}, u32[]{:S(2)}, u32[]{:S(2)}) collective-permute-start(f32[2,264,128]{2,1,0:T(8,128)} %get-tuple-element.14), channel_id=1, source_target_pairs={{0,3},{1,0},{2,1},{3,2},{4,7},{5,4},{6,5},{7,6},{8,11},{9,8},{10,9... | collective-permute-start | bytes 811016 | tf_op jit(solution)/shard_map/ppermute | solution.py:322
  27.0 0.0 collective-permute-start.3
  27.0 0.0 collective-permute-done
  27.1 1.0 %add.27 = f32[2,264,128]{2,1,0:T(8,128)S(1)} add(f32[2,264,128]{2,1,0:T(8,128)} %get-tuple-element.12, f32[2,264,128]{2,1,0:T(8,128)S(1)} %collective-permute-done) | non-fusion elementwise | flops 67584 | bytes 811008 | tf_op jit(solution)/shard_map/add | solution.py:323
  28.0 0.1 collective-permute-start.1
  28.1 0.0 collective-permute-done.4
  28.1 1.7 %add.28 = f32[2,264,128]{2,1,0:T(8,128)} add(f32[2,264,128]{2,1,0:T(8,128)} %get-tuple-element.16, f32[2,264,128]{2,1,0:T(8,128)S(1)} %collective-permute-done.4) | non-fusion elementwise | flops 67584 | bytes 811008 | tf_op jit(solution)/shard_map/add | solution.py:323
  29.8 3.2 %collective-permute-start.5 = (f32[2,264,128]{2,1,0:T(8,128)}, f32[2,264,128]{2,1,0:T(8,128)S(1)}, u32[]{:S(2)}, u32[]{:S(2)}) collective-permute-start(f32[2,264,128]{2,1,0:T(8,128)} %add.28), channel_id=1, source_target_pairs={{0,3},{1,0},{2,1},{3,2},{4,7},{5,4},{6,5},{7,6},{8,11},{9,8},{10,9... | collective-permute-start | bytes 811016 | tf_op jit(solution)/shard_map/ppermute | solution.py:323
  33.1 0.0 copy-done
  33.1 0.2 collective-permute-done.2.b1
  33.3 4.6 %collective-permute-done.3.a0 = f32[2,264,128]{2,1,0:T(8,128)S(1)} collective-permute-done((f32[2,264,128]{2,1,0:T(8,128)}, f32[2,264,128]{2,1,0:T(8,128)S(1)}, u32[]{:S(2)}, u32[]{:S(2)}) %collective-permute-start.3) | collective-permute-done | bytes 270368 | tf_op jit(solution)/shard_map/ppermute | solution.py:322
  37.9 3.4 %collective-permute-done.1.b0 = f32[2,264,128]{2,1,0:T(8,128)S(1)} collective-permute-done((f32[2,264,128]{2,1,0:T(8,128)S(1)}, f32[2,264,128]{2,1,0:T(8,128)S(1)}, u32[]{:S(2)}, u32[]{:S(2)}) %collective-permute-start.1) | collective-permute-done | bytes 270368 | tf_op jit(solution)/shard_map/ppermute | solution.py:323
  41.3 0.0 collective-permute-done.5.a1
  41.3 0.0 copy-done.1
  41.3 0.0 copy-done.2
  41.3 9.5 %factor_scenes.1 = (f32[4,192,256]{2,1,0:T(8,128)}, f32[64,64]{1,0:T(8,128)S(1)}) custom-call(f32[4]{0:T(128)S(1)} %copy-done.2, f32[4,264,128]{2,1,0:T(8,128)S(1)} %copy-done.1, f32[2,264,128]{2,1,0:T(8,128)S(1)} %collective-permute-done.1.b0, f32[2,264,128]{2,1,0:T(8,128)S(1)} %collective-permute-done.2.b1, f32[2,264,128]{2,1,0:T(8,128)S(1)} %collective-permute-done.3.a0, ...), custom_call_target="tpu_custom_call" | custom-call | tf_op jit(solution)/shard_map/factor_scenes/pallas_call | solution.py:157
  50.8 0.0 collective-permute-start.6
  50.8 1.2 %collective-permute-done.6 = f32[64,64]{1,0:T(8,128)S(1)} collective-permute-done((f32[64,64]{1,0:T(8,128)S(1)}, f32[64,64]{1,0:T(8,128)S(1)}, u32[]{:S(2)}, u32[]{:S(2)}) %collective-permute-start.6) | collective-permute-done | bytes 16416 | tf_op jit(solution)/shard_map/ppermute | solution.py:329
  52.0 0.0 collective-permute-start.7
  52.0 3.9 %collective-permute-done.7 = f32[64,64]{1,0:T(8,128)S(1)} collective-permute-done((f32[64,64]{1,0:T(8,128)S(1)}, f32[64,64]{1,0:T(8,128)S(1)}, u32[]{:S(2)}, u32[]{:S(2)}) %collective-permute-start.7) | collective-permute-done | bytes 16416 | tf_op jit(solution)/shard_map/ppermute | solution.py:329
  55.9 0.4 collective-permute-start.8
  56.2 4.8 %collective-permute-done.8 = f32[64,64]{1,0:T(8,128)S(1)} collective-permute-done((f32[64,64]{1,0:T(8,128)S(1)}, f32[64,64]{1,0:T(8,128)S(1)}, u32[]{:S(2)}, u32[]{:S(2)}) %collective-permute-start.8) | collective-permute-done | bytes 16416 | tf_op jit(solution)/shard_map/ppermute | solution.py:329
  61.0 1.6 %collective-permute-start.9 = (f32[64,64]{1,0:T(8,128)S(1)}, f32[64,64]{1,0:T(8,128)S(1)}, u32[]{:S(2)}, u32[]{:S(2)}) collective-permute-start(f32[64,64]{1,0:T(8,128)S(1)} %add.32), channel_id=1, source_target_pairs={{0,8},{4,12},{8,0},{12,4},{16,24},{20,28},{24,16},{28,20},{32,40},... | collective-permute-start | bytes 49160 | tf_op jit(solution)/shard_map/ppermute | solution.py:329
  62.6 2.3 %collective-permute-done.9 = f32[64,64]{1,0:T(8,128)S(1)} collective-permute-done((f32[64,64]{1,0:T(8,128)S(1)}, f32[64,64]{1,0:T(8,128)S(1)}, u32[]{:S(2)}, u32[]{:S(2)}) %collective-permute-start.9) | collective-permute-done | bytes 16416 | tf_op jit(solution)/shard_map/ppermute | solution.py:329
  64.9 4.4 %collective-permute-start.10 = (f32[64,64]{1,0:T(8,128)S(1)}, f32[64,64]{1,0:T(8,128)S(1)}, u32[]{:S(2)}, u32[]{:S(2)}) collective-permute-start(f32[64,64]{1,0:T(8,128)S(1)} %add.33), channel_id=1, source_target_pairs={{0,24},{4,28},{8,16},{12,20},{16,8},{20,12},{24,0},{28,4},{32,56},... | collective-permute-start | bytes 49160 | tf_op jit(solution)/shard_map/ppermute | solution.py:329
  69.3 1.9 %collective-permute-done.10 = f32[64,64]{1,0:T(8,128)S(1)} collective-permute-done((f32[64,64]{1,0:T(8,128)S(1)}, f32[64,64]{1,0:T(8,128)S(1)}, u32[]{:S(2)}, u32[]{:S(2)}) %collective-permute-start.10) | collective-permute-done | bytes 16416 | tf_op jit(solution)/shard_map/ppermute | solution.py:329
  71.2 0.4 collective-permute-start.11
  71.7 3.5 %collective-permute-done.11 = f32[64,64]{1,0:T(8,128)S(1)} collective-permute-done((f32[64,64]{1,0:T(8,128)S(1)}, f32[64,64]{1,0:T(8,128)S(1)}, u32[]{:S(2)}, u32[]{:S(2)}) %collective-permute-start.11) | collective-permute-done | bytes 16416 | tf_op jit(solution)/shard_map/ppermute | solution.py:329
  75.2 0.0 copy-start.3
  75.2 2.5 %collective-permute-start.12 = (f32[64,64]{1,0:T(8,128)S(1)}, f32[64,64]{1,0:T(8,128)S(1)}, u32[]{:S(2)}, u32[]{:S(2)}) collective-permute-start(f32[64,64]{1,0:T(8,128)S(1)} %add.35.refs_1_), channel_id=1, source_target_pairs={{0,96},{4,100},{8,104},{12,108},{16,112},{20,116},{24,120},{28,124... | collective-permute-start | bytes 49160 | tf_op jit(solution)/shard_map/ppermute | solution.py:330
  77.6 2.7 %collective-permute-done.12.refs_2_ = f32[64,64]{1,0:T(8,128)S(1)} collective-permute-done((f32[64,64]{1,0:T(8,128)S(1)}, f32[64,64]{1,0:T(8,128)S(1)}, u32[]{:S(2)}, u32[]{:S(2)}) %collective-permute-start.12) | collective-permute-done | bytes 16416 | tf_op jit(solution)/shard_map/ppermute | solution.py:330
  80.4 0.0 copy-start.4
  80.4 0.0 copy-done.3
  80.4 0.6 copy-done.4
  81.0 3.2 %factor_total.1 = f32[64,64]{1,0:T(8,128)} custom-call(f32[1,64]{1,0:T(1,128)} %bitcast.2, f32[64,64]{1,0:T(8,128)} %copy-done.3, f32[64,64]{1,0:T(8,128)} %copy-done.4), custom_call_target="tpu_custom_call" | custom-call | tf_op jit(solution)/shard_map/factor_total/pallas_call | solution.py:199
  (7 shorter events, 0.1 us)
Async XLA Ops:
  0.6 32.4 %copy-start = (bf16[16,192,192]{2,1,0:T(8,128)(2,1)S(1)}, bf16[16,192,192]{2,1,0:T(8,128)(2,1)}, u32[]{:S(2)}) copy-start(bf16[16,192,192]{2,1,0:T(8,128)(2,1)} %param.9) | copy-start | bytes 3538948
  7.4 19.6 %collective-permute-start = (f32[2,264,128]{2,1,0:T(8,128)}, f32[2,264,128]{2,1,0:T(8,128)S(1)}, u32[]{:S(2)}, u32[]{:S(2)}) collective-permute-start(f32[2,264,128]{2,1,0:T(8,128)} %get-tuple-element.13), channel_id=1, source_target_pairs={{0,1},{1,2},{2,3},{3,0},{4,5},{5,6},{6,7},{7,4},{8,9},{9,10},{10,1... | collective-permute-start | bytes 811016 | tf_op jit(solution)/shard_map/ppermute | solution.py:316
  8.5 19.7 %collective-permute-start.4 = (f32[2,264,128]{2,1,0:T(8,128)}, f32[2,264,128]{2,1,0:T(8,128)S(1)}, u32[]{:S(2)}, u32[]{:S(2)}) collective-permute-start(f32[2,264,128]{2,1,0:T(8,128)} %get-tuple-element.17), channel_id=1, source_target_pairs={{0,3},{1,0},{2,1},{3,2},{4,7},{5,4},{6,5},{7,6},{8,11},{9,8},{10,9... | collective-permute-start | bytes 811016 | tf_op jit(solution)/shard_map/ppermute | solution.py:316
  23.6 17.7 %copy-start.1 = (f32[4,264,128]{2,1,0:T(8,128)S(1)}, f32[4,264,128]{2,1,0:T(8,128)}, u32[]{:S(2)}) copy-start(f32[4,264,128]{2,1,0:T(8,128)} %get-tuple-element.11.own_ref) | copy-start | bytes 1622020
  23.6 17.6 %copy-start.2 = (f32[4]{0:T(128)S(1)}, f32[4]{0:T(128)}, u32[]{:S(2)}) copy-start(f32[4]{0:T(128)} %damp_ref.1) | copy-start | bytes 52
  23.7 9.6 %collective-permute-start.2 = (f32[2,264,128]{2,1,0:T(8,128)}, f32[2,264,128]{2,1,0:T(8,128)S(1)}, u32[]{:S(2)}, u32[]{:S(2)}) collective-permute-start(f32[2,264,128]{2,1,0:T(8,128)} %get-tuple-element.14), channel_id=1, source_target_pairs={{0,3},{1,0},{2,1},{3,2},{4,7},{5,4},{6,5},{7,6},{8,11},{9,8},{10,9... | collective-permute-start | bytes 811016 | tf_op jit(solution)/shard_map/ppermute | solution.py:322
  27.0 10.8 %collective-permute-start.3 = (f32[2,264,128]{2,1,0:T(8,128)}, f32[2,264,128]{2,1,0:T(8,128)S(1)}, u32[]{:S(2)}, u32[]{:S(2)}) collective-permute-start(f32[2,264,128]{2,1,0:T(8,128)} %get-tuple-element.15), channel_id=1, source_target_pairs={{0,1},{1,2},{2,3},{3,0},{4,5},{5,6},{6,7},{7,4},{8,9},{9,10},{10,1... | collective-permute-start | bytes 811016 | tf_op jit(solution)/shard_map/ppermute | solution.py:322
  28.0 13.2 %collective-permute-start.1 = (f32[2,264,128]{2,1,0:T(8,128)S(1)}, f32[2,264,128]{2,1,0:T(8,128)S(1)}, u32[]{:S(2)}, u32[]{:S(2)}) collective-permute-start(f32[2,264,128]{2,1,0:T(8,128)S(1)} %add.27), channel_id=1, source_target_pairs={{0,1},{1,2},{2,3},{3,0},{4,5},{5,6},{6,7},{7,4},{8,9},{9,10},{10,1... | collective-permute-start | bytes 811016 | tf_op jit(solution)/shard_map/ppermute | solution.py:323
  29.8 11.5 %collective-permute-start.5 = (f32[2,264,128]{2,1,0:T(8,128)}, f32[2,264,128]{2,1,0:T(8,128)S(1)}, u32[]{:S(2)}, u32[]{:S(2)}) collective-permute-start(f32[2,264,128]{2,1,0:T(8,128)} %add.28), channel_id=1, source_target_pairs={{0,3},{1,0},{2,1},{3,2},{4,7},{5,4},{6,5},{7,6},{8,11},{9,8},{10,9... | collective-permute-start | bytes 811016 | tf_op jit(solution)/shard_map/ppermute | solution.py:323
  50.8 1.2 %collective-permute-start.6 = (f32[64,64]{1,0:T(8,128)S(1)}, f32[64,64]{1,0:T(8,128)S(1)}, u32[]{:S(2)}, u32[]{:S(2)}) collective-permute-start(f32[64,64]{1,0:T(8,128)S(1)} %get-tuple-element.19), channel_id=1, source_target_pairs={{0,4},{4,0},{8,12},{12,8},{16,20},{20,16},{24,28},{28,24},{32,36},... | collective-permute-start | bytes 49160 | tf_op jit(solution)/shard_map/ppermute | solution.py:329
  52.0 3.9 %collective-permute-start.7 = (f32[64,64]{1,0:T(8,128)S(1)}, f32[64,64]{1,0:T(8,128)S(1)}, u32[]{:S(2)}, u32[]{:S(2)}) collective-permute-start(f32[64,64]{1,0:T(8,128)S(1)} %add.30), channel_id=1, source_target_pairs={{0,1},{1,0},{2,3},{3,2},{4,5},{5,4},{6,7},{7,6},{8,9},{9,8},{10,11... | collective-permute-start | bytes 49160 | tf_op jit(solution)/shard_map/ppermute | solution.py:329
  55.9 5.1 %collective-permute-start.8 = (f32[64,64]{1,0:T(8,128)S(1)}, f32[64,64]{1,0:T(8,128)S(1)}, u32[]{:S(2)}, u32[]{:S(2)}) collective-permute-start(f32[64,64]{1,0:T(8,128)S(1)} %add.31), channel_id=1, source_target_pairs={{0,3},{1,2},{2,1},{3,0},{4,7},{5,6},{6,5},{7,4},{8,11},{9,10},{10,... | collective-permute-start | bytes 49160 | tf_op jit(solution)/shard_map/ppermute | solution.py:329
  61.0 3.9 %collective-permute-start.9 = (f32[64,64]{1,0:T(8,128)S(1)}, f32[64,64]{1,0:T(8,128)S(1)}, u32[]{:S(2)}, u32[]{:S(2)}) collective-permute-start(f32[64,64]{1,0:T(8,128)S(1)} %add.32), channel_id=1, source_target_pairs={{0,8},{4,12},{8,0},{12,4},{16,24},{20,28},{24,16},{28,20},{32,40},... | collective-permute-start | bytes 49160 | tf_op jit(solution)/shard_map/ppermute | solution.py:329
  64.9 6.3 %collective-permute-start.10 = (f32[64,64]{1,0:T(8,128)S(1)}, f32[64,64]{1,0:T(8,128)S(1)}, u32[]{:S(2)}, u32[]{:S(2)}) collective-permute-start(f32[64,64]{1,0:T(8,128)S(1)} %add.33), channel_id=1, source_target_pairs={{0,24},{4,28},{8,16},{12,20},{16,8},{20,12},{24,0},{28,4},{32,56},... | collective-permute-start | bytes 49160 | tf_op jit(solution)/shard_map/ppermute | solution.py:329
  71.2 3.9 %collective-permute-start.11 = (f32[64,64]{1,0:T(8,128)S(1)}, f32[64,64]{1,0:T(8,128)S(1)}, u32[]{:S(2)}, u32[]{:S(2)}) collective-permute-start(f32[64,64]{1,0:T(8,128)S(1)} %add.34), channel_id=1, source_target_pairs={{0,32},{4,36},{8,40},{12,44},{16,48},{20,52},{24,56},{28,60},{32,0... | collective-permute-start | bytes 49160 | tf_op jit(solution)/shard_map/ppermute | solution.py:329
  75.2 5.2 %copy-start.3 = (f32[64,64]{1,0:T(8,128)}, f32[64,64]{1,0:T(8,128)S(1)}, u32[]{:S(2)}) copy-start(f32[64,64]{1,0:T(8,128)S(1)} %add.35.refs_1_) | copy-start | bytes 49156
  75.2 5.2 %collective-permute-start.12 = (f32[64,64]{1,0:T(8,128)S(1)}, f32[64,64]{1,0:T(8,128)S(1)}, u32[]{:S(2)}, u32[]{:S(2)}) collective-permute-start(f32[64,64]{1,0:T(8,128)S(1)} %add.35.refs_1_), channel_id=1, source_target_pairs={{0,96},{4,100},{8,104},{12,108},{16,112},{20,116},{24,120},{28,124... | collective-permute-start | bytes 49160 | tf_op jit(solution)/shard_map/ppermute | solution.py:330
  80.4 0.6 copy-start.4

commit v2 on v1

--- a/solution.py
+++ b/solution.py
@@ -13,8 +13,9 @@
 PACK = 264
 PANEL = 32
 N_PANEL = SPLINE // PANEL
-UNROLL = 4
-DEPTH = 16
+UNROLL = 8
+DEPTH = 32
+WORD = 24
 f32 = jnp.float32
 bf16 = jnp.bfloat16
 
@@ -110,7 +111,6 @@
         info = info + jnp.where(iota((SPLINE, COLS), 0) == iota((SPLINE, COLS), 1), damp_ref[s], 0.0)
         for p in range(N_PANEL):
             work[p, s * PANEL:(s + 1) * PANEL] = info[p * PANEL:(p + 1) * PANEL]
-    tail_sum = tail_sum[:, SHARED:]
 
     lane = iota((PANEL, 128), 1)
     same = (r1 // PANEL) == (c1 // PANEL)
@@ -143,8 +143,8 @@
         cross_high, cross_low = high[:, 128:], low[:, 128:]
         both = ((0,), (0,))
         outer = dot(cross_high, cross_high, both) + (dot(cross_high, cross_low, both) + dot(cross_low, cross_high, both))
-        tail_sum = tail_sum - outer[SHARED:, SHARED:]
-    sum_ref[...] = tail_sum
+        tail_sum = tail_sum - outer[SHARED:]
+    sum_ref[...] = jnp.where(lane < SHARED, pltpu.roll(tail_sum[:PANEL], SHARED, 1), tail_sum[PANEL:])
 
 
 def factor_scenes(own, below, above, sens, damping):
@@ -158,7 +158,7 @@
         kernel,
         out_shape=(
             jax.ShapeDtypeStruct((owned, SPLINE, COLS), f32),
-            jax.ShapeDtypeStruct((SHARED, SHARED), f32),
+            jax.ShapeDtypeStruct((PANEL, 128), f32),
         ),
         in_specs=[pl.BlockSpec(memory_space=pltpu.SMEM)] + [vmem] * 6,
         out_specs=(vmem, vmem),
@@ -168,28 +168,22 @@
     )(damping, own, *below, *above, sens)
 
 
-def total_kernel(n_parts, count, *refs):
-    prior_ref = refs[0]
-    out_ref = refs[-1]
-    total = refs[1][...]
-    for other in refs[2:-1]:
-        total = total + other[...]
+def total_kernel(count, prior_ref, parts_ref, out_ref):
+    total = parts_ref[0]
+    for i in range(1, parts_ref.shape[0]):
+        total = total + parts_ref[i]
     total = total / count
-    r, c = iota((SHARED, SHARED), 0), iota((SHARED, SHARED), 1)
-    total = total + jnp.where(r == c, prior_ref[...], 0.0)
-    pad = jnp.zeros((SHARED, 128 - SHARED), f32)
-    wide = jnp.concatenate([total, pad], 1)
-    top, bottom = wide[:PANEL], wide[PANEL:]
-    lane = iota((PANEL, 128), 1)
-    row = iota((PANEL, 128), 0)
-    inverse = invert_lower(top)
-    upper = dot3(jnp.where(lane < PANEL, inverse, 0.0)[:, :PANEL], top)
-    upper = jnp.where(lane >= row, upper, 0.0)
+    lane, row = iota((PANEL, 128), 1), iota((PANEL, 128), 0)
+    prior = jnp.concatenate([prior_ref[...], prior_ref[...]], 1)
+    total = total + jnp.where((lane == row) | (lane == row + SHARED + PANEL), prior, 0.0)
+    first = jnp.where(lane < PANEL, invert_lower(total), 0.0)
+    upper = dot3(first[:, :PANEL], total)
+    upper = jnp.where((lane >= row) & (lane < SHARED), upper, 0.0)
+    bottom = pltpu.roll(total, SHARED, 1)
     high, low = split(upper)
-    bottom = bottom - outer_panel(high, low, high, low)[PANEL:SHARED]
-    moved = pltpu.roll(bottom, 128 - PANEL, 1)
-    inverse = invert_lower(moved)
-    lower = dot3(inverse[:, :PANEL], bottom)
+    bottom = jnp.where(lane < SHARED, bottom - outer_panel(high, low, high, low)[PANEL:SHARED], 0.0)
+    second = jnp.where(lane < PANEL, invert_lower(pltpu.roll(bottom, 128 - PANEL, 1)), 0.0)
+    lower = dot3(second[:, :PANEL], bottom)
     lower = jnp.where(lane >= row + PANEL, lower, 0.0)
     out_ref[...] = jnp.concatenate([upper[:, :SHARED], lower[:, :SHARED]], 0)
 
@@ -197,51 +191,60 @@
 def factor_total(parts, prior, count):
     vmem = pl.BlockSpec(memory_space=pltpu.VMEM)
     return pl.pallas_call(
-        functools.partial(total_kernel, len(parts), count),
+        functools.partial(total_kernel, count),
         out_shape=jax.ShapeDtypeStruct((SHARED, SHARED), f32),
-        in_specs=[vmem] * (1 + len(parts)),
+        in_specs=[vmem] * 2,
         out_specs=vmem,
         name="factor_total",
-    )(prior.reshape(1, SHARED), *parts)
-
-
-def gram_kernel(groups, me_ref, pat_ref, cnt_ref, tie_ref, *rest):
+    )(prior.reshape(1, SHARED), parts)
+
+
+def gram_kernel(groups, n_begin, me_ref, bits_ref, cnt_ref, tie_ref, *rest):
     n_out = len(groups)
+    begin_refs, rest = rest[:n_begin], rest[n_begin:]
     outs = rest[:n_out]
     acc, held, pairs, sems = rest[n_out:]
-    n_block = tie_ref.shape[0]
     slots = [(distance, scene) for distance, scenes in groups for scene in scenes]
     n_slot = len(slots)
     ways = 4
+    rings = DEPTH // UNROLL
+
+    def fetch(block, slot):
+        return pltpu.make_async_copy(tie_ref.at[block], held.at[slot], sems.at[slot])
+
+    def note(found, pair):
+        pairs[found] = pair
+
+        @pl.when(found < DEPTH)
+        def _():
+            fetch(lax.bitwise_and(pair, 1023), found).start()
+
     found = jnp.int32(0)
     for slot, (distance, scene) in enumerate(slots):
-        row = lax.rem(me_ref[0] + distance, ways) * (pat_ref.shape[0] // ways) + scene
-
-        def some(i, found, slot=slot, row=row):
-            for j in range(8):
-                block = i * 8 + j
-                pairs[found] = slot * 1024 + block
-                found = found + pat_ref[row, block]
-            return found
-
-        found = lax.fori_loop(0, n_block // 8, some, found)
-    for j in range(UNROLL):
-        pairs[found + j] = n_slot * 1024
+        row = lax.rem(me_ref[0] + distance, ways) * (bits_ref.shape[1] // ways) + scene
+        for w in range(bits_ref.shape[0]):
+
+            def some(carry, slot=slot, w=w):
+                word, found = carry
+                low = lax.bitwise_and(word, -word)
+                note(found, slot * 1024 + w * WORD + 31 - lax.clz(low))
+                return word - low, found + 1
+
+            _, found = lax.while_loop(lambda carry: carry[0] != 0, some, (bits_ref[w, row], found))
     rounds = lax.div(found + (UNROLL - 1), UNROLL)
-    rings = DEPTH // UNROLL
-
-    def fetch(index, slot):
-        return pltpu.make_async_copy(
-            tie_ref.at[lax.bitwise_and(pairs[index], 1023)], held.at[slot], sems.at[slot]
-        )
-
-    for g in range(rings):
-        @pl.when(g < rounds)
-        def _():
-            for j in range(UNROLL):
-                fetch(g * UNROLL + j, g * UNROLL + j).start()
-
-    acc[...] = jnp.zeros_like(acc)
+    for j in range(UNROLL - 1):
+        @pl.when(found + j < rounds * UNROLL)
+        def _(j=j):
+            note(found + j, n_slot * 1024)
+
+    if n_begin:
+        at = 0
+        for begin_ref in begin_refs:
+            acc[at:at + begin_ref.shape[0]] = begin_ref[...]
+            at += begin_ref.shape[0]
+        acc[at] = jnp.zeros_like(acc[at])
+    else:
+        acc[...] = jnp.zeros_like(acc)
     row_at = iota((COLS, COLS), 0)
     r1, c1 = iota((128, 128), 0), iota((128, 128), 1)
     both = ((0,), (0,))
@@ -249,7 +252,7 @@
     def step(i, carry):
         base = lax.rem(i, rings) * UNROLL
         for j in range(UNROLL):
-            fetch(i * UNROLL + j, base + j).wait()
+            fetch(0, base + j).wait()
         for j in range(UNROLL):
             pair = pairs[i * UNROLL + j]
             slot = lax.shift_right_logical(pair, 10)
@@ -264,7 +267,7 @@
         @pl.when(i + rings < rounds)
         def _():
             for j in range(UNROLL):
-                fetch((i + rings) * UNROLL + j, base + j).start()
+                fetch(lax.bitwise_and(pairs[(i + rings) * UNROLL + j], 1023), base + j).start()
         return carry
 
     lax.fori_loop(0, rounds, step, 0)
@@ -274,15 +277,15 @@
         at += len(scenes)
 
 
-def partial_grams(me, pattern, counts, tie_rows, groups):
+def partial_grams(me, bits, counts, tie_rows, groups, begin=()):
     smem = pl.BlockSpec(memory_space=pltpu.SMEM)
     vmem = pl.BlockSpec(memory_space=pltpu.VMEM)
     n_slot = sum(len(scenes) for _, scenes in groups)
     n_pairs = n_slot * tie_rows.shape[0] + UNROLL
     return pl.pallas_call(
-        functools.partial(gram_kernel, groups),
+        functools.partial(gram_kernel, groups, len(begin)),
         out_shape=[jax.ShapeDtypeStruct((len(scenes), PACK, 128), f32) for _, scenes in groups],
-        in_specs=[smem, smem, smem, pl.BlockSpec(memory_space=pl.ANY)],
+        in_specs=[smem, smem, smem, pl.BlockSpec(memory_space=pl.ANY)] + [vmem] * len(begin),
         out_specs=[vmem] * len(groups),
         scratch_shapes=[
             pltpu.VMEM((n_slot + 1, PACK, 128), f32),
@@ -290,17 +293,27 @@
             pltpu.SMEM(((n_pairs + 127) // 128 * 128,), jnp.int32),
             pltpu.SemaphoreType.DMA((DEPTH,)),
         ],
-        compiler_params=pltpu.CompilerParams(vmem_limit_bytes=56 * 1024 * 1024),
+        compiler_params=pltpu.CompilerParams(vmem_limit_bytes=52 * 1024 * 1024),
         name="partial_grams",
-    )(me, pattern, counts, tie_rows)
+    )(me, bits, counts, tie_rows, *begin)
+
+
+def pattern_bits(pattern):
+    n_scene, n_block = pattern.shape
+    words = -(-n_block // WORD)
+    block = jnp.arange(n_block, dtype=jnp.int32)
+    bit = jnp.left_shift(1, block % WORD)
+    weight = jnp.where(block[None, :] // WORD == jnp.arange(words, dtype=jnp.int32)[:, None], bit[None, :], 0)
+    return jnp.sum(pattern[None, :, :] * weight[:, None, :], axis=2)
 
 
 def ring(step, size):
     return [(i, (i + step) % size) for i in range(size)]
 
 
-def swap(bits, size):
-    return [(i, i ^ bits) for i in range(size)]
+def share(value, axes, groups):
+    sent = jnp.broadcast_to(value[None], (len(groups[0]),) + value.shape)
+    return lax.all_to_all(sent, axes, 0, 0, axis_index_groups=groups, tiled=True)
 
 
 def on_device(tie_rows, point_counts, pattern, sensitivity, damping, prior):
@@ -312,23 +325,26 @@
     up = functools.partial(lax.ppermute, axis_name="tie", perm=ring(1, ways))
     down = functools.partial(lax.ppermute, axis_name="tie", perm=ring(-1, ways))
 
-    far_up, far_down = partial_grams(me_word, pattern, point_counts, tie_rows, ((2, near), (2, far)))
+    bits = pattern_bits(pattern)
+    far_up, far_down = partial_grams(me_word, bits, point_counts, tie_rows, ((2, near), (2, far)))
     came_up, came_down = up(far_up), down(far_down)
-    up_now, up_later, down_now, down_later, own = partial_grams(
-        me_word, pattern, point_counts, tie_rows,
-        ((1, far), (1, near), (3, near), (3, far), (0, near + far)),
-    )
+    up_now, down_now = partial_grams(me_word, bits, point_counts, tie_rows, ((1, far), (3, near)))
     sens = lax.dynamic_slice_in_dim(sensitivity, me * owned, owned, 0)
     got_up, got_down = up(up_now), down(down_now)
-    last_up, last_down = up(up_later + came_up), down(down_later + came_down)
+    up_later, down_later = partial_grams(
+        me_word, bits, point_counts, tie_rows, ((1, near), (3, far)), (came_up, came_down)
+    )
+    last_up, last_down = up(up_later), down(down_later)
+    (own,) = partial_grams(me_word, bits, point_counts, tie_rows, ((0, near + far),))
     scene_rows, reduced = factor_scenes(own, (last_up, got_down), (got_up, last_down), sens, damping)
 
     n_scene = lax.axis_size("scene")
-    total = reduced
-    for axis, bits in (("scene", 1), ("tie", 1), ("tie", 3), ("scene", 2), ("scene", 6), ("scene", 8)):
-        total = total + lax.ppermute(total, axis, swap(bits, lax.axis_size(axis)))
-    other = lax.ppermute(total, "scene", swap(24, n_scene))
-    global_factor = factor_total((total, other), prior, float(owned * n_scene * ways))
+    plane = [[i for i in range(n_scene) if i % 2 == core] for core in range(2)]
+    line = [list(range(ways))]
+    chip = reduced + lax.ppermute(reduced, "scene", [(i, i ^ 1) for i in range(n_scene)])
+    shares = share(chip, "scene", plane)
+    total_parts = share(jnp.sum(shares, 0), "tie", line)
+    global_factor = factor_total(total_parts, prior, float(owned * n_scene * ways))
     return (scene_rows, global_factor)
 
 

time: 84.7 us -> 72.2 us (0.85)
  blocking collectives: 0 us -> 26 us
  waiting for transfers between devices: 28.6 us -> 4.13 us
  starting transfers between devices: 19.2 us -> 9.79 us
  Pallas kernels: 32.3 us -> 29.6 us
  other arithmetic: 2.7 us -> 0.99 us
    all_to_all x0 -> x2, blocking collectives: none -> 26 us  [share(): lax.all_to_all(sent, axes, 0, 0, axis_index_groups=groups, tiled=True)]
    ppermute x9 -> x3, waiting for transfers between devices: 23.8 us -> 4.12 us  [the longest x2 2.94 us: on_device(): last_up, last_down = (up(up_later), down(down_later))]
    ppermute x9 -> x3, starting transfers between devices: 12.5 us -> 3.94 us  [the longest x2 3.94 us: on_device(): last_up, last_down = (up(up_later), down(down_later))]
    ppermute x2, waiting for transfers between devices: 4.8 us -> 0.01 us  [on_device(): got_up, got_down = (up(up_now), down(down_now))]
    pallas_call x3 -> x5, Pallas kernels: 22.9 us -> 20.1 us  [the longest x4 16.8 us: partial_grams(): pl.pallas_call(functools.partial(gram_kernel, groups, len(begin)), out_sh...]
    add x8 -> x1, other arithmetic: 2.7 us -> 0.01 us  [on_device(): reduced + lax.ppermute(reduced, 'scene', [(i, i ^ 1) for i in range(n_sce...]
    reduce_sum x0 -> x2, other arithmetic: none -> 0.97 us  [the longest x1 0.95 us: pattern_bits(): return jnp.sum(pattern[None, :, :] * weight[:, None, :], axis=2)]
  transfers between devices with their start and end apart: 13 -> 7, of which waited for: 10 -> 2; matrix products, arithmetic and copies ran while one was open for 3% -> 0% of each run, Pallas kernels for 15% -> 18%
where the time goes in v2:
time: 72.2 us; the launch traced here: 72 us
  Pallas kernels  29.6 us (41%)
  blocking collectives  26 us (36%)
  starting transfers between devices  9.79 us (14%)
  waiting for transfers between devices  4.13 us (6%)
  other arithmetic  0.99 us (1%)
  between operations  0.76 us (1%)
  local copies, waits for them, and re-layouts  0.73 us (1%)
    all_to_all x2, blocking collectives, share(): lax.all_to_all(sent, axes, 0, 0, axis_index_groups=groups, tiled=True)  26 us
    pallas_call x4, Pallas kernels, partial_grams(): pl.pallas_call(functools.partial(gram_kernel, groups, len(begin)), out_sh...  16.8 us
    pallas_call x1, Pallas kernels, factor_scenes(): pl.pallas_call(kernel, out_shape=(jax.ShapeDtypeStruct((owned, SPLINE, CO...  9.46 us
    ppermute x2, starting transfers between devices, on_device(): last_up, last_down = (up(up_later), down(down_later))  3.94 us
    ppermute x2, starting transfers between devices, on_device(): came_up, came_down = (up(far_up), down(far_down))  3.31 us
    pallas_call x1, Pallas kernels, factor_total(): pl.pallas_call(functools.partial(total_kernel, count), out_shape=jax.Shap...  3.28 us
    ppermute x2, waiting for transfers between devices, on_device(): last_up, last_down = (up(up_later), down(down_later))  2.94 us
    ppermute x2, starting transfers between devices, on_device(): got_up, got_down = (up(up_now), down(down_now))  2.54 us
  transfers between devices with their start and end apart: 7, of which 2 were waited for; matrix products, arithmetic and copies ran while one was open for 0% of the time, Pallas kernels for 18%

profile of v2, /device:TPU:0, one launch (start us, length us, event | category | flops | bytes accessed | tf_op | source)
XLA Modules:
  0.0 72.0 jit_solution(1088475769111755509)
XLA Ops:
  0.6 0.0 copy-start
  0.7 0.9 %multiply_reduce_fusion.bits_ref = s32[4,16]{1,0:T(4,128)S(1)} fusion(s32[4,96]{1,0:T(4,128)S(1)} %fusion, s32[16,96]{1,0:T(8,128)} %param.8), kind=kLoop, calls=%fused_computation | loop fusion | flops 12224 | bytes 7936 | tf_op jit(solution)/shard_map/reduce_sum | solution.py:307
  1.6 0.0 copy-start.1
  1.6 0.7 copy-done.1
  2.3 3.8 %partial_grams.5 = (f32[2,264,128]{2,1,0:T(8,128)S(1)}, f32[2,264,128]{2,1,0:T(8,128)S(1)}) custom-call(s32[1]{0:T(128)} %bitcast.me_ref, s32[4,16]{1,0:T(4,128)S(1)} %multiply_reduce_fusion.bits_ref, s32[96]{0:T(128)S(1)} %copy-done.1, bf16[96,256,256]{2,1,0:T(8,128)(2,1)} %tie_ref.7), custom_call_target="tpu_custom_call" | custom-call | tf_op jit(solution)/shard_map/partial_grams/pallas_call | solution.py:285
  6.1 1.7 %collective-permute-start = (f32[2,264,128]{2,1,0:T(8,128)S(1)}, f32[2,264,128]{2,1,0:T(8,128)S(1)}, u32[]{:S(2)}, u32[]{:S(2)}) collective-permute-start(f32[2,264,128]{2,1,0:T(8,128)S(1)} %get-tuple-element.10), channel_id=1, source_target_pairs={{0,1},{1,2},{2,3},{3,0},{4,5},{5,6},{6,7},{7,4},{8,9},{9,10},{10,1... | collective-permute-start | bytes 811016 | tf_op jit(solution)/shard_map/ppermute | solution.py:330
  7.9 1.6 %collective-permute-start.1 = (f32[2,264,128]{2,1,0:T(8,128)S(1)}, f32[2,264,128]{2,1,0:T(8,128)S(1)}, u32[]{:S(2)}, u32[]{:S(2)}) collective-permute-start(f32[2,264,128]{2,1,0:T(8,128)S(1)} %get-tuple-element.11), channel_id=1, source_target_pairs={{0,3},{1,0},{2,1},{3,2},{4,7},{5,4},{6,5},{7,6},{8,11},{9,8},{10,9... | collective-permute-start | bytes 811016 | tf_op jit(solution)/shard_map/ppermute | solution.py:330
  9.4 4.5 %partial_grams.7 = (f32[2,264,128]{2,1,0:T(8,128)S(1)}, f32[2,264,128]{2,1,0:T(8,128)}) custom-call(s32[1]{0:T(128)} %bitcast.me_ref, s32[4,16]{1,0:T(4,128)S(1)} %multiply_reduce_fusion.bits_ref, s32[96]{0:T(128)S(1)} %copy-done.1, bf16[96,256,256]{2,1,0:T(8,128)(2,1)} %tie_ref.7), custom_call_target="tpu_custom_call" | custom-call | tf_op jit(solution)/shard_map/partial_grams/pallas_call | solution.py:285
  14.0 2.5 %collective-permute-start.3 = (f32[2,264,128]{2,1,0:T(8,128)}, f32[2,264,128]{2,1,0:T(8,128)S(1)}, u32[]{:S(2)}, u32[]{:S(2)}) collective-permute-start(f32[2,264,128]{2,1,0:T(8,128)} %get-tuple-element.13), channel_id=1, source_target_pairs={{0,3},{1,0},{2,1},{3,2},{4,7},{5,4},{6,5},{7,6},{8,11},{9,8},{10,9... | collective-permute-start | bytes 811016 | tf_op jit(solution)/shard_map/ppermute | solution.py:333
  16.5 0.0 collective-permute-start.4
  16.5 0.0 collective-permute-done.rest_0_
  16.5 0.0 collective-permute-done.1.rest_1_
  16.5 4.1 %partial_grams.6 = (f32[2,264,128]{2,1,0:T(8,128)}, f32[2,264,128]{2,1,0:T(8,128)}) custom-call(s32[1]{0:T(128)} %bitcast.me_ref, s32[4,16]{1,0:T(4,128)S(1)} %multiply_reduce_fusion.bits_ref, s32[96]{0:T(128)S(1)} %copy-done.1, bf16[96,256,256]{2,1,0:T(8,128)(2,1)} %tie_ref.7, f32[2,264,128]{2,1,0:T(8,128)S(1)} %collective-permute-done.rest_0_, ...), custom_call_target="tpu_custom_call" | custom-call | tf_op jit(solution)/shard_map/partial_grams/pallas_call | solution.py:285
  20.6 2.0 %collective-permute-start.2 = (f32[2,264,128]{2,1,0:T(8,128)}, f32[2,264,128]{2,1,0:T(8,128)S(1)}, u32[]{:S(2)}, u32[]{:S(2)}) collective-permute-start(f32[2,264,128]{2,1,0:T(8,128)} %get-tuple-element.12), channel_id=1, source_target_pairs={{0,1},{1,2},{2,3},{3,0},{4,5},{5,6},{6,7},{7,4},{8,9},{9,10},{10,1... | collective-permute-start | bytes 811016 | tf_op jit(solution)/shard_map/ppermute | solution.py:337
  22.7 0.0 copy-start.2
  22.7 1.9 %collective-permute-start.5 = (f32[2,264,128]{2,1,0:T(8,128)}, f32[2,264,128]{2,1,0:T(8,128)S(1)}, u32[]{:S(2)}, u32[]{:S(2)}) collective-permute-start(f32[2,264,128]{2,1,0:T(8,128)} %get-tuple-element.15), channel_id=1, source_target_pairs={{0,3},{1,0},{2,1},{3,2},{4,7},{5,4},{6,5},{7,6},{8,11},{9,8},{10,9... | collective-permute-start | bytes 811016 | tf_op jit(solution)/shard_map/ppermute | solution.py:337
  24.6 4.4 %partial_grams.4.own_ref = f32[4,264,128]{2,1,0:T(8,128)S(1)} custom-call(s32[1]{0:T(128)} %bitcast.me_ref, s32[4,16]{1,0:T(4,128)S(1)} %multiply_reduce_fusion.bits_ref, s32[96]{0:T(128)S(1)} %copy-done.1, bf16[96,256,256]{2,1,0:T(8,128)(2,1)} %tie_ref.7), custom_call_target="tpu_custom_call" | custom-call | tf_op jit(solution)/shard_map/partial_grams/pallas_call | solution.py:285
  29.0 0.0 copy-done
  29.0 0.0 collective-permute-done.3.b1
  29.0 0.0 collective-permute-done.4.a0
  29.0 2.9 %collective-permute-done.2.b0 = f32[2,264,128]{2,1,0:T(8,128)S(1)} collective-permute-done((f32[2,264,128]{2,1,0:T(8,128)}, f32[2,264,128]{2,1,0:T(8,128)S(1)}, u32[]{:S(2)}, u32[]{:S(2)}) %collective-permute-start.2) | collective-permute-done | bytes 270368 | tf_op jit(solution)/shard_map/ppermute | solution.py:337
  32.0 0.0 collective-permute-done.5.a1
  32.0 0.0 copy-done.2
  32.0 9.5 %factor_scenes.1 = (f32[4,192,256]{2,1,0:T(8,128)}, f32[32,128]{1,0:T(8,128)S(1)}) custom-call(f32[4]{0:T(128)S(1)} %copy-done.2, f32[4,264,128]{2,1,0:T(8,128)S(1)} %partial_grams.4.own_ref, f32[2,264,128]{2,1,0:T(8,128)S(1)} %collective-permute-done.2.b0, f32[2,264,128]{2,1,0:T(8,128)S(1)} %collective-permute-done.3.b1, ...), custom_call_target="tpu_custom_call" | custom-call | tf_op jit(solution)/shard_map/factor_scenes/pallas_call | solution.py:157
  41.4 0.0 collective-permute-start.6
  41.4 1.2 %collective-permute-done.6 = f32[32,128]{1,0:T(8,128)S(1)} collective-permute-done((f32[32,128]{1,0:T(8,128)S(1)}, f32[32,128]{1,0:T(8,128)S(1)}, u32[]{:S(2)}, u32[]{:S(2)}) %collective-permute-start.6) | collective-permute-done | bytes 16416 | tf_op jit(solution)/shard_map/ppermute | solution.py:344
  42.7 16.3 %all_to_all.10 = f32[16,32,128]{2,1,0:T(8,128)S(1)} all-to-all(f32[16,32,128]{2,1,0:T(8,128)S(1)} %broadcast_in_dim.18), channel_id=1, replica_groups={{0,8,16,24,32,40,48,56,64,72,80,88,96,104,112,120},{4,12,20,28,36,44,52..., dimensions={0} | all-to-all | bytes 524288 | tf_op jit(solution)/shard_map/all_to_all | solution.py:316
  59.0 9.8 %all_to_all.11.parts_ref = f32[4,32,128]{2,1,0:T(8,128)} all-to-all(f32[4,32,128]{2,1,0:T(8,128)S(1)} %broadcast_in_dim.19), channel_id=1, replica_groups={{0,1,2,3},{4,5,6,7},{8,9,10,11},{12,13,14,15},{16,17,18,19},{20,21,22,2..., dimensions={0} | all-to-all | bytes 131072 | tf_op jit(solution)/shard_map/all_to_all | solution.py:316
  68.7 3.3 %factor_total.1 = f32[64,64]{1,0:T(8,128)} custom-call(f32[1,64]{1,0:T(1,128)} %bitcast.2, f32[4,32,128]{2,1,0:T(8,128)} %all_to_all.11.parts_ref), custom_call_target="tpu_custom_call" | custom-call | tf_op jit(solution)/shard_map/factor_total/pallas_call | solution.py:193
  (7 shorter events, 0.1 us)
Async XLA Ops:
  0.6 28.3 %copy-start = (bf16[16,192,192]{2,1,0:T(8,128)(2,1)S(1)}, bf16[16,192,192]{2,1,0:T(8,128)(2,1)}, u32[]{:S(2)}) copy-start(bf16[16,192,192]{2,1,0:T(8,128)(2,1)} %param.9) | copy-start | bytes 3538948
  1.6 0.7 copy-start.1
  6.1 10.4 %collective-permute-start = (f32[2,264,128]{2,1,0:T(8,128)S(1)}, f32[2,264,128]{2,1,0:T(8,128)S(1)}, u32[]{:S(2)}, u32[]{:S(2)}) collective-permute-start(f32[2,264,128]{2,1,0:T(8,128)S(1)} %get-tuple-element.10), channel_id=1, source_target_pairs={{0,1},{1,2},{2,3},{3,0},{4,5},{5,6},{6,7},{7,4},{8,9},{9,10},{10,1... | collective-permute-start | bytes 811016 | tf_op jit(solution)/shard_map/ppermute | solution.py:330
  7.9 8.6 %collective-permute-start.1 = (f32[2,264,128]{2,1,0:T(8,128)S(1)}, f32[2,264,128]{2,1,0:T(8,128)S(1)}, u32[]{:S(2)}, u32[]{:S(2)}) collective-permute-start(f32[2,264,128]{2,1,0:T(8,128)S(1)} %get-tuple-element.11), channel_id=1, source_target_pairs={{0,3},{1,0},{2,1},{3,2},{4,7},{5,4},{6,5},{7,6},{8,11},{9,8},{10,9... | collective-permute-start | bytes 811016 | tf_op jit(solution)/shard_map/ppermute | solution.py:330
  14.0 15.0 %collective-permute-start.3 = (f32[2,264,128]{2,1,0:T(8,128)}, f32[2,264,128]{2,1,0:T(8,128)S(1)}, u32[]{:S(2)}, u32[]{:S(2)}) collective-permute-start(f32[2,264,128]{2,1,0:T(8,128)} %get-tuple-element.13), channel_id=1, source_target_pairs={{0,3},{1,0},{2,1},{3,2},{4,7},{5,4},{6,5},{7,6},{8,11},{9,8},{10,9... | collective-permute-start | bytes 811016 | tf_op jit(solution)/shard_map/ppermute | solution.py:333
  16.5 12.5 %collective-permute-start.4 = (f32[2,264,128]{2,1,0:T(8,128)S(1)}, f32[2,264,128]{2,1,0:T(8,128)S(1)}, u32[]{:S(2)}, u32[]{:S(2)}) collective-permute-start(f32[2,264,128]{2,1,0:T(8,128)S(1)} %get-tuple-element.14), channel_id=1, source_target_pairs={{0,1},{1,2},{2,3},{3,0},{4,5},{5,6},{6,7},{7,4},{8,9},{9,10},{10,1... | collective-permute-start | bytes 811016 | tf_op jit(solution)/shard_map/ppermute | solution.py:333
  20.6 11.4 %collective-permute-start.2 = (f32[2,264,128]{2,1,0:T(8,128)}, f32[2,264,128]{2,1,0:T(8,128)S(1)}, u32[]{:S(2)}, u32[]{:S(2)}) collective-permute-start(f32[2,264,128]{2,1,0:T(8,128)} %get-tuple-element.12), channel_id=1, source_target_pairs={{0,1},{1,2},{2,3},{3,0},{4,5},{5,6},{6,7},{7,4},{8,9},{9,10},{10,1... | collective-permute-start | bytes 811016 | tf_op jit(solution)/shard_map/ppermute | solution.py:337
  22.7 9.3 %copy-start.2 = (f32[4]{0:T(128)S(1)}, f32[4]{0:T(128)}, u32[]{:S(2)}) copy-start(f32[4]{0:T(128)} %damp_ref.1) | copy-start | bytes 52
  22.7 9.3 %collective-permute-start.5 = (f32[2,264,128]{2,1,0:T(8,128)}, f32[2,264,128]{2,1,0:T(8,128)S(1)}, u32[]{:S(2)}, u32[]{:S(2)}) collective-permute-start(f32[2,264,128]{2,1,0:T(8,128)} %get-tuple-element.15), channel_id=1, source_target_pairs={{0,3},{1,0},{2,1},{3,2},{4,7},{5,4},{6,5},{7,6},{8,11},{9,8},{10,9... | collective-permute-start | bytes 811016 | tf_op jit(solution)/shard_map/ppermute | solution.py:337
  41.4 1.2 %collective-permute-start.6 = (f32[32,128]{1,0:T(8,128)S(1)}, f32[32,128]{1,0:T(8,128)S(1)}, u32[]{:S(2)}, u32[]{:S(2)}) collective-permute-start(f32[32,128]{1,0:T(8,128)S(1)} %get-tuple-element.17), channel_id=1, source_target_pairs={{0,4},{4,0},{8,12},{12,8},{16,20},{20,16},{24,28},{28,24},{32,36},... | collective-permute-start | bytes 49160 | tf_op jit(solution)/shard_map/ppermute | solution.py:344

commit v3 on v2

--- a/solution.py
+++ b/solution.py
@@ -60,24 +60,26 @@
     def spread(block, at):
         return jnp.broadcast_to(block[at:at + 1], (8, 128))
 
+    scales = [jnp.ones((8, 128), f32) for _ in range(blocks)]
     for k in range(PANEL):
         kv, ks = divmod(k, 8)
-        scale = lax.rsqrt(spread(columns[k][kv], ks))
-        lower = [None] * blocks
-        for v in range(kv, blocks):
-            lower[v] = columns[k][v] * scale
+        pivot = spread(columns[k][kv], ks)
+        inverse = 1.0 / pivot
+        scales[kv] = jnp.where(sub == ks, lax.rsqrt(pivot), scales[kv])
+        lower = [None] * kv + [columns[k][v] * inverse for v in range(kv, blocks)]
         for j in range(k + 1, PANEL):
             jv, js = divmod(j, 8)
-            factor = spread(lower[jv], js)
+            factor = spread(columns[k][jv], js)
             for v in range(jv, blocks):
-                columns[j][v] = columns[j][v] - lower[v] * factor
-        row = spread(x[kv], ks) * scale
+                if j == k + 1:
+                    columns[j][v] = columns[j][v] - (columns[k][v] * factor) * inverse
+                else:
+                    columns[j][v] = columns[j][v] - lower[v] * factor
+        row = spread(x[kv], ks)
         for v in range(kv, blocks):
-            if v == kv:
-                below = jnp.where(sub > ks, lower[v], 0.0)
-                x[v] = jnp.where(sub == ks, row, x[v] - below * row)
-            else:
-                x[v] = x[v] - lower[v] * row
+            below = jnp.where(sub > ks, lower[v], 0.0) if v == kv else lower[v]
+            x[v] = x[v] - below * row
+    x = [value * scale for value, scale in zip(x, scales)]
     return jnp.concatenate(x, 0)
 
 
@@ -195,6 +197,7 @@
         out_shape=jax.ShapeDtypeStruct((SHARED, SHARED), f32),
         in_specs=[vmem] * 2,
         out_specs=vmem,
+        compiler_params=pltpu.CompilerParams(vmem_limit_bytes=8 * 1024 * 1024),
         name="factor_total",
     )(prior.reshape(1, SHARED), parts)
 

time: 72.2 us -> 70.5 us (0.976)
  waiting for transfers between devices: 4.13 us -> 3.03 us
  starting transfers between devices: 9.79 us -> 8.71 us
    ppermute x2, waiting for transfers between devices: 2.94 us -> 1.83 us  [on_device(): last_up, last_down = (up(up_later), down(down_later))]
    pallas_call x4, Pallas kernels: 16.8 us -> 17.9 us  [partial_grams(): pl.pallas_call(functools.partial(gram_kernel, groups, len(begin)), out_sh...]
    pallas_call x1, Pallas kernels: 3.28 us -> 2.42 us  [factor_total(): pl.pallas_call(functools.partial(total_kernel, count), out_shape=jax.Shap...]
  transfers between devices with their start and end apart: 7 -> 7, of which waited for: 2 -> 2; matrix products, arithmetic and copies ran while one was open for 0% -> 0% of each run, Pallas kernels for 18% -> 19%
where the time goes in v3:
time: 70.5 us; the launch traced here: 70.1 us
  Pallas kernels  29.4 us (42%)
  blocking collectives  26.4 us (37%)
  starting transfers between devices  8.71 us (12%)
  waiting for transfers between devices  3.03 us (4%)
  other arithmetic  0.99 us (1%)
  between operations  0.77 us (1%)
  local copies, waits for them, and re-layouts  0.74 us (1%)
    all_to_all x2, blocking collectives, share(): lax.all_to_all(sent, axes, 0, 0, axis_index_groups=groups, tiled=True)  26.4 us
    pallas_call x4, Pallas kernels, partial_grams(): pl.pallas_call(functools.partial(gram_kernel, groups, len(begin)), out_sh...  17.9 us
    pallas_call x1, Pallas kernels, factor_scenes(): pl.pallas_call(kernel, out_shape=(jax.ShapeDtypeStruct((owned, SPLINE, CO...  9.1 us
    ppermute x2, starting transfers between devices, on_device(): came_up, came_down = (up(far_up), down(far_down))  3.31 us
    ppermute x2, starting transfers between devices, on_device(): last_up, last_down = (up(up_later), down(down_later))  3.31 us
    pallas_call x1, Pallas kernels, factor_total(): pl.pallas_call(functools.partial(total_kernel, count), out_shape=jax.Shap...  2.42 us
    ppermute x2, starting transfers between devices, on_device(): got_up, got_down = (up(up_now), down(down_now))  2.09 us
    ppermute x2, waiting for transfers between devices, on_device(): last_up, last_down = (up(up_later), down(down_later))  1.83 us
  transfers between devices with their start and end apart: 7, of which 2 were waited for; matrix products, arithmetic and copies ran while one was open for 0% of the time, Pallas kernels for 19%

profile of v3, /device:TPU:0, one launch (start us, length us, event | category | flops | bytes accessed | tf_op | source)
XLA Modules:
  0.0 70.1 jit_solution(5702188687432901465)
XLA Ops:
  0.6 0.0 copy-start
  0.7 0.9 %multiply_reduce_fusion.bits_ref = s32[4,16]{1,0:T(4,128)S(1)} fusion(s32[4,96]{1,0:T(4,128)S(1)} %fusion, s32[16,96]{1,0:T(8,128)} %param.8), kind=kLoop, calls=%fused_computation | loop fusion | flops 12224 | bytes 7936 | tf_op jit(solution)/shard_map/reduce_sum | solution.py:310
  1.6 0.0 copy-start.1
  1.6 0.7 copy-done.1
  2.3 4.4 %partial_grams.5 = (f32[2,264,128]{2,1,0:T(8,128)S(1)}, f32[2,264,128]{2,1,0:T(8,128)S(1)}) custom-call(s32[1]{0:T(128)} %bitcast.me_ref, s32[4,16]{1,0:T(4,128)S(1)} %multiply_reduce_fusion.bits_ref, s32[96]{0:T(128)S(1)} %copy-done.1, bf16[96,256,256]{2,1,0:T(8,128)(2,1)} %tie_ref.7), custom_call_target="tpu_custom_call" | custom-call | tf_op jit(solution)/shard_map/partial_grams/pallas_call | solution.py:288
  6.7 1.2 %collective-permute-start = (f32[2,264,128]{2,1,0:T(8,128)S(1)}, f32[2,264,128]{2,1,0:T(8,128)S(1)}, u32[]{:S(2)}, u32[]{:S(2)}) collective-permute-start(f32[2,264,128]{2,1,0:T(8,128)S(1)} %get-tuple-element.10), channel_id=1, source_target_pairs={{0,1},{1,2},{2,3},{3,0},{4,5},{5,6},{6,7},{7,4},{8,9},{9,10},{10,1... | collective-permute-start | bytes 811016 | tf_op jit(solution)/shard_map/ppermute | solution.py:333
  7.9 2.1 %collective-permute-start.1 = (f32[2,264,128]{2,1,0:T(8,128)S(1)}, f32[2,264,128]{2,1,0:T(8,128)S(1)}, u32[]{:S(2)}, u32[]{:S(2)}) collective-permute-start(f32[2,264,128]{2,1,0:T(8,128)S(1)} %get-tuple-element.11), channel_id=1, source_target_pairs={{0,3},{1,0},{2,1},{3,2},{4,7},{5,4},{6,5},{7,6},{8,11},{9,8},{10,9... | collective-permute-start | bytes 811016 | tf_op jit(solution)/shard_map/ppermute | solution.py:333
  10.0 5.1 %partial_grams.7 = (f32[2,264,128]{2,1,0:T(8,128)S(1)}, f32[2,264,128]{2,1,0:T(8,128)}) custom-call(s32[1]{0:T(128)} %bitcast.me_ref, s32[4,16]{1,0:T(4,128)S(1)} %multiply_reduce_fusion.bits_ref, s32[96]{0:T(128)S(1)} %copy-done.1, bf16[96,256,256]{2,1,0:T(8,128)(2,1)} %tie_ref.7), custom_call_target="tpu_custom_call" | custom-call | tf_op jit(solution)/shard_map/partial_grams/pallas_call | solution.py:288
  15.1 0.9 %collective-permute-start.3 = (f32[2,264,128]{2,1,0:T(8,128)}, f32[2,264,128]{2,1,0:T(8,128)S(1)}, u32[]{:S(2)}, u32[]{:S(2)}) collective-permute-start(f32[2,264,128]{2,1,0:T(8,128)} %get-tuple-element.13), channel_id=1, source_target_pairs={{0,3},{1,0},{2,1},{3,2},{4,7},{5,4},{6,5},{7,6},{8,11},{9,8},{10,9... | collective-permute-start | bytes 811016 | tf_op jit(solution)/shard_map/ppermute | solution.py:336
  15.9 1.2 %collective-permute-start.4 = (f32[2,264,128]{2,1,0:T(8,128)S(1)}, f32[2,264,128]{2,1,0:T(8,128)S(1)}, u32[]{:S(2)}, u32[]{:S(2)}) collective-permute-start(f32[2,264,128]{2,1,0:T(8,128)S(1)} %get-tuple-element.14), channel_id=1, source_target_pairs={{0,1},{1,2},{2,3},{3,0},{4,5},{5,6},{6,7},{7,4},{8,9},{9,10},{10,1... | collective-permute-start | bytes 811016 | tf_op jit(solution)/shard_map/ppermute | solution.py:336
  17.2 0.0 collective-permute-done.rest_0_
  17.2 0.0 collective-permute-done.1.rest_1_
  17.2 4.6 %partial_grams.6 = (f32[2,264,128]{2,1,0:T(8,128)}, f32[2,264,128]{2,1,0:T(8,128)}) custom-call(s32[1]{0:T(128)} %bitcast.me_ref, s32[4,16]{1,0:T(4,128)S(1)} %multiply_reduce_fusion.bits_ref, s32[96]{0:T(128)S(1)} %copy-done.1, bf16[96,256,256]{2,1,0:T(8,128)(2,1)} %tie_ref.7, f32[2,264,128]{2,1,0:T(8,128)S(1)} %collective-permute-done.rest_0_, ...), custom_call_target="tpu_custom_call" | custom-call | tf_op jit(solution)/shard_map/partial_grams/pallas_call | solution.py:288
  21.8 0.5 collective-permute-start.2
  22.3 0.0 copy-start.2
  22.3 2.8 %collective-permute-start.5 = (f32[2,264,128]{2,1,0:T(8,128)}, f32[2,264,128]{2,1,0:T(8,128)S(1)}, u32[]{:S(2)}, u32[]{:S(2)}) collective-permute-start(f32[2,264,128]{2,1,0:T(8,128)} %get-tuple-element.15), channel_id=1, source_target_pairs={{0,3},{1,0},{2,1},{3,2},{4,7},{5,4},{6,5},{7,6},{8,11},{9,8},{10,9... | collective-permute-start | bytes 811016 | tf_op jit(solution)/shard_map/ppermute | solution.py:340
  25.1 3.8 %partial_grams.4.own_ref = f32[4,264,128]{2,1,0:T(8,128)S(1)} custom-call(s32[1]{0:T(128)} %bitcast.me_ref, s32[4,16]{1,0:T(4,128)S(1)} %multiply_reduce_fusion.bits_ref, s32[96]{0:T(128)S(1)} %copy-done.1, bf16[96,256,256]{2,1,0:T(8,128)(2,1)} %tie_ref.7), custom_call_target="tpu_custom_call" | custom-call | tf_op jit(solution)/shard_map/partial_grams/pallas_call | solution.py:288
  29.0 0.0 copy-done
  29.0 0.0 copy-start.3
  29.0 0.0 collective-permute-done.3.b1
  29.0 0.0 collective-permute-done.4.a0
  29.1 1.8 %collective-permute-done.2.b0 = f32[2,264,128]{2,1,0:T(8,128)S(1)} collective-permute-done((f32[2,264,128]{2,1,0:T(8,128)}, f32[2,264,128]{2,1,0:T(8,128)S(1)}, u32[]{:S(2)}, u32[]{:S(2)}) %collective-permute-start.2) | collective-permute-done | bytes 270368 | tf_op jit(solution)/shard_map/ppermute | solution.py:340
  30.9 0.0 collective-permute-done.5.a1
  30.9 0.0 copy-done.2
  30.9 9.1 %factor_scenes.1 = (f32[4,192,256]{2,1,0:T(8,128)}, f32[32,128]{1,0:T(8,128)S(1)}) custom-call(f32[4]{0:T(128)S(1)} %copy-done.2, f32[4,264,128]{2,1,0:T(8,128)S(1)} %partial_grams.4.own_ref, f32[2,264,128]{2,1,0:T(8,128)S(1)} %collective-permute-done.2.b0, f32[2,264,128]{2,1,0:T(8,128)S(1)} %collective-permute-done.3.b1, ...), custom_call_target="tpu_custom_call" | custom-call | tf_op jit(solution)/shard_map/factor_scenes/pallas_call | solution.py:159
  40.0 0.0 collective-permute-start.6
  40.0 1.2 %collective-permute-done.6 = f32[32,128]{1,0:T(8,128)S(1)} collective-permute-done((f32[32,128]{1,0:T(8,128)S(1)}, f32[32,128]{1,0:T(8,128)S(1)}, u32[]{:S(2)}, u32[]{:S(2)}) %collective-permute-start.6) | collective-permute-done | bytes 16416 | tf_op jit(solution)/shard_map/ppermute | solution.py:347
  41.2 16.9 %all_to_all.10 = f32[16,32,128]{2,1,0:T(8,128)S(1)} all-to-all(f32[16,32,128]{2,1,0:T(8,128)S(1)} %broadcast_in_dim.18), channel_id=1, replica_groups={{0,8,16,24,32,40,48,56,64,72,80,88,96,104,112,120},{4,12,20,28,36,44,52..., dimensions={0} | all-to-all | bytes 524288 | tf_op jit(solution)/shard_map/all_to_all | solution.py:319
  58.1 9.6 %all_to_all.11.parts_ref = f32[4,32,128]{2,1,0:T(8,128)S(1)} all-to-all(f32[4,32,128]{2,1,0:T(8,128)S(1)} %broadcast_in_dim.19), channel_id=1, replica_groups={{0,1,2,3},{4,5,6,7},{8,9,10,11},{12,13,14,15},{16,17,18,19},{20,21,22,2..., dimensions={0} | all-to-all | bytes 131072 | tf_op jit(solution)/shard_map/all_to_all | solution.py:319
  67.7 0.0 copy-done.3
  67.7 2.4 %factor_total.1 = f32[64,64]{1,0:T(8,128)} custom-call(f32[1,64]{1,0:T(1,128)S(1)} %bitcast.2, f32[4,32,128]{2,1,0:T(8,128)S(1)} %all_to_all.11.parts_ref), custom_call_target="tpu_custom_call" | custom-call | tf_op jit(solution)/shard_map/factor_total/pallas_call | solution.py:195
  (7 shorter events, 0.1 us)
Async XLA Ops:
  0.6 28.3 %copy-start = (bf16[16,192,192]{2,1,0:T(8,128)(2,1)S(1)}, bf16[16,192,192]{2,1,0:T(8,128)(2,1)}, u32[]{:S(2)}) copy-start(bf16[16,192,192]{2,1,0:T(8,128)(2,1)} %param.9) | copy-start | bytes 3538948
  1.6 0.7 copy-start.1
  6.7 10.5 %collective-permute-start = (f32[2,264,128]{2,1,0:T(8,128)S(1)}, f32[2,264,128]{2,1,0:T(8,128)S(1)}, u32[]{:S(2)}, u32[]{:S(2)}) collective-permute-start(f32[2,264,128]{2,1,0:T(8,128)S(1)} %get-tuple-element.10), channel_id=1, source_target_pairs={{0,1},{1,2},{2,3},{3,0},{4,5},{5,6},{6,7},{7,4},{8,9},{9,10},{10,1... | collective-permute-start | bytes 811016 | tf_op jit(solution)/shard_map/ppermute | solution.py:333
  7.9 9.3 %collective-permute-start.1 = (f32[2,264,128]{2,1,0:T(8,128)S(1)}, f32[2,264,128]{2,1,0:T(8,128)S(1)}, u32[]{:S(2)}, u32[]{:S(2)}) collective-permute-start(f32[2,264,128]{2,1,0:T(8,128)S(1)} %get-tuple-element.11), channel_id=1, source_target_pairs={{0,3},{1,0},{2,1},{3,2},{4,7},{5,4},{6,5},{7,6},{8,11},{9,8},{10,9... | collective-permute-start | bytes 811016 | tf_op jit(solution)/shard_map/ppermute | solution.py:333
  15.1 14.0 %collective-permute-start.3 = (f32[2,264,128]{2,1,0:T(8,128)}, f32[2,264,128]{2,1,0:T(8,128)S(1)}, u32[]{:S(2)}, u32[]{:S(2)}) collective-permute-start(f32[2,264,128]{2,1,0:T(8,128)} %get-tuple-element.13), channel_id=1, source_target_pairs={{0,3},{1,0},{2,1},{3,2},{4,7},{5,4},{6,5},{7,6},{8,11},{9,8},{10,9... | collective-permute-start | bytes 811016 | tf_op jit(solution)/shard_map/ppermute | solution.py:336
  15.9 13.1 %collective-permute-start.4 = (f32[2,264,128]{2,1,0:T(8,128)S(1)}, f32[2,264,128]{2,1,0:T(8,128)S(1)}, u32[]{:S(2)}, u32[]{:S(2)}) collective-permute-start(f32[2,264,128]{2,1,0:T(8,128)S(1)} %get-tuple-element.14), channel_id=1, source_target_pairs={{0,1},{1,2},{2,3},{3,0},{4,5},{5,6},{6,7},{7,4},{8,9},{9,10},{10,1... | collective-permute-start | bytes 811016 | tf_op jit(solution)/shard_map/ppermute | solution.py:336
  21.8 9.1 %collective-permute-start.2 = (f32[2,264,128]{2,1,0:T(8,128)}, f32[2,264,128]{2,1,0:T(8,128)S(1)}, u32[]{:S(2)}, u32[]{:S(2)}) collective-permute-start(f32[2,264,128]{2,1,0:T(8,128)} %get-tuple-element.12), channel_id=1, source_target_pairs={{0,1},{1,2},{2,3},{3,0},{4,5},{5,6},{6,7},{7,4},{8,9},{9,10},{10,1... | collective-permute-start | bytes 811016 | tf_op jit(solution)/shard_map/ppermute | solution.py:340
  22.3 8.6 %copy-start.2 = (f32[4]{0:T(128)S(1)}, f32[4]{0:T(128)}, u32[]{:S(2)}) copy-start(f32[4]{0:T(128)} %damp_ref.1) | copy-start | bytes 52
  22.3 8.6 %collective-permute-start.5 = (f32[2,264,128]{2,1,0:T(8,128)}, f32[2,264,128]{2,1,0:T(8,128)S(1)}, u32[]{:S(2)}, u32[]{:S(2)}) collective-permute-start(f32[2,264,128]{2,1,0:T(8,128)} %get-tuple-element.15), channel_id=1, source_target_pairs={{0,3},{1,0},{2,1},{3,2},{4,7},{5,4},{6,5},{7,6},{8,11},{9,8},{10,9... | collective-permute-start | bytes 811016 | tf_op jit(solution)/shard_map/ppermute | solution.py:340
  29.0 38.7 %copy-start.3 = (f32[64]{0:T(128)S(1)}, f32[64]{0:T(128)}, u32[]{:S(2)}) copy-start(f32[64]{0:T(128)} %param.11) | copy-start | bytes 772
  40.0 1.2 %collective-permute-start.6 = (f32[32,128]{1,0:T(8,128)S(1)}, f32[32,128]{1,0:T(8,128)S(1)}, u32[]{:S(2)}, u32[]{:S(2)}) collective-permute-start(f32[32,128]{1,0:T(8,128)S(1)} %get-tuple-element.17), channel_id=1, source_target_pairs={{0,4},{4,0},{8,12},{12,8},{16,20},{20,16},{24,28},{28,24},{32,36},... | collective-permute-start | bytes 49160 | tf_op jit(solution)/shard_map/ppermute | solution.py:347

commit v4 on v3

--- a/solution.py
+++ b/solution.py
@@ -146,7 +146,14 @@
         both = ((0,), (0,))
         outer = dot(cross_high, cross_high, both) + (dot(cross_high, cross_low, both) + dot(cross_low, cross_high, both))
         tail_sum = tail_sum - outer[SHARED:]
-    sum_ref[...] = jnp.where(lane < SHARED, pltpu.roll(tail_sum[:PANEL], SHARED, 1), tail_sum[PANEL:])
+    whole = jnp.where(lane[:16] < SHARED, pltpu.roll(tail_sum[:16], SHARED, 1), tail_sum[16:PANEL])
+    last = jnp.zeros((8, 128), f32)
+    for i in range(4):
+        piece = tail_sum[PANEL + 8 * i:PANEL + 8 * i + 8]
+        if i < 3:
+            piece = pltpu.roll(piece, PANEL * (i + 1), 1)
+        last = jnp.where(lane[:8] // PANEL == i, piece, last)
+    sum_ref[...] = jnp.concatenate([whole, last], 0)
 
 
 def factor_scenes(own, below, above, sens, damping):
@@ -160,7 +167,7 @@
         kernel,
         out_shape=(
             jax.ShapeDtypeStruct((owned, SPLINE, COLS), f32),
-            jax.ShapeDtypeStruct((PANEL, 128), f32),
+            jax.ShapeDtypeStruct((24, 128), f32),
         ),
         in_specs=[pl.BlockSpec(memory_space=pltpu.SMEM)] + [vmem] * 6,
         out_specs=(vmem, vmem),
@@ -177,13 +184,14 @@
     total = total / count
     lane, row = iota((PANEL, 128), 1), iota((PANEL, 128), 0)
     prior = jnp.concatenate([prior_ref[...], prior_ref[...]], 1)
-    total = total + jnp.where((lane == row) | (lane == row + SHARED + PANEL), prior, 0.0)
+    last = [total[16:24] if i == 1 else pltpu.roll(total[16:24], (PANEL - PANEL * i) % 128, 1) for i in range(4)]
+    bottom = jnp.concatenate(last, 0) + jnp.where(lane == row + PANEL, prior, 0.0)
+    total = jnp.concatenate([total[:16], pltpu.roll(total[:16], SHARED, 1)], 0) + jnp.where(lane == row, prior, 0.0)
     first = jnp.where(lane < PANEL, invert_lower(total), 0.0)
     upper = dot3(first[:, :PANEL], total)
     upper = jnp.where((lane >= row) & (lane < SHARED), upper, 0.0)
-    bottom = pltpu.roll(total, SHARED, 1)
     high, low = split(upper)
-    bottom = jnp.where(lane < SHARED, bottom - outer_panel(high, low, high, low)[PANEL:SHARED], 0.0)
+    bottom = jnp.where((lane >= PANEL) & (lane < SHARED), bottom - outer_panel(high, low, high, low)[PANEL:SHARED], 0.0)
     second = jnp.where(lane < PANEL, invert_lower(pltpu.roll(bottom, 128 - PANEL, 1)), 0.0)
     lower = dot3(second[:, :PANEL], bottom)
     lower = jnp.where(lane >= row + PANEL, lower, 0.0)

time: 70.5 us -> 70.2 us (level)
  no operation moved by 1% of the time
where the time goes in v4:
time: 70.2 us; the launch traced here: 69.7 us
  Pallas kernels  29.5 us (42%)
  blocking collectives  26 us (37%)
  starting transfers between devices  9.22 us (13%)
  waiting for transfers between devices  2.47 us (4%)
  other arithmetic  0.99 us (1%)
  between operations  0.77 us (1%)
  local copies, waits for them, and re-layouts  0.73 us (1%)
    all_to_all x2, blocking collectives, share(): lax.all_to_all(sent, axes, 0, 0, axis_index_groups=groups, tiled=True)  26 us
    pallas_call x4, Pallas kernels, partial_grams(): pl.pallas_call(functools.partial(gram_kernel, groups, len(begin)), out_sh...  18 us
    pallas_call x1, Pallas kernels, factor_scenes(): pl.pallas_call(kernel, out_shape=(jax.ShapeDtypeStruct((owned, SPLINE, CO...  9.11 us
    ppermute x2, starting transfers between devices, on_device(): came_up, came_down = (up(far_up), down(far_down))  3.82 us
    ppermute x2, starting transfers between devices, on_device(): last_up, last_down = (up(up_later), down(down_later))  3.31 us
    pallas_call x1, Pallas kernels, factor_total(): pl.pallas_call(functools.partial(total_kernel, count), out_shape=jax.Shap...  2.43 us
    ppermute x2, starting transfers between devices, on_device(): got_up, got_down = (up(up_now), down(down_now))  2.09 us
  transfers between devices with their start and end apart: 7, of which 2 were waited for; matrix products, arithmetic and copies ran while one was open for 0% of the time, Pallas kernels for 19%

profile of v4, /device:TPU:0, one launch (start us, length us, event | category | flops | bytes accessed | tf_op | source)
XLA Modules:
  0.0 69.7 jit_solution(11908375112096558995)
XLA Ops:
  0.6 0.0 copy-start
  0.7 0.9 %multiply_reduce_fusion.bits_ref = s32[4,16]{1,0:T(4,128)S(1)} fusion(s32[4,96]{1,0:T(4,128)S(1)} %fusion, s32[16,96]{1,0:T(8,128)} %param.8), kind=kLoop, calls=%fused_computation | loop fusion | flops 12224 | bytes 7936 | tf_op jit(solution)/shard_map/reduce_sum | solution.py:318
  1.6 0.0 copy-start.1
  1.6 0.7 copy-done.1
  2.3 4.4 %partial_grams.5 = (f32[2,264,128]{2,1,0:T(8,128)S(1)}, f32[2,264,128]{2,1,0:T(8,128)S(1)}) custom-call(s32[1]{0:T(128)} %bitcast.me_ref, s32[4,16]{1,0:T(4,128)S(1)} %multiply_reduce_fusion.bits_ref, s32[96]{0:T(128)S(1)} %copy-done.1, bf16[96,256,256]{2,1,0:T(8,128)(2,1)} %tie_ref.7), custom_call_target="tpu_custom_call" | custom-call | tf_op jit(solution)/shard_map/partial_grams/pallas_call | solution.py:296
  6.7 1.2 %collective-permute-start = (f32[2,264,128]{2,1,0:T(8,128)S(1)}, f32[2,264,128]{2,1,0:T(8,128)S(1)}, u32[]{:S(2)}, u32[]{:S(2)}) collective-permute-start(f32[2,264,128]{2,1,0:T(8,128)S(1)} %get-tuple-element.10), channel_id=1, source_target_pairs={{0,1},{1,2},{2,3},{3,0},{4,5},{5,6},{6,7},{7,4},{8,9},{9,10},{10,1... | collective-permute-start | bytes 811016 | tf_op jit(solution)/shard_map/ppermute | solution.py:341
  7.9 2.6 %collective-permute-start.1 = (f32[2,264,128]{2,1,0:T(8,128)S(1)}, f32[2,264,128]{2,1,0:T(8,128)S(1)}, u32[]{:S(2)}, u32[]{:S(2)}) collective-permute-start(f32[2,264,128]{2,1,0:T(8,128)S(1)} %get-tuple-element.11), channel_id=1, source_target_pairs={{0,3},{1,0},{2,1},{3,2},{4,7},{5,4},{6,5},{7,6},{8,11},{9,8},{10,9... | collective-permute-start | bytes 811016 | tf_op jit(solution)/shard_map/ppermute | solution.py:341
  10.5 4.5 %partial_grams.7 = (f32[2,264,128]{2,1,0:T(8,128)S(1)}, f32[2,264,128]{2,1,0:T(8,128)}) custom-call(s32[1]{0:T(128)} %bitcast.me_ref, s32[4,16]{1,0:T(4,128)S(1)} %multiply_reduce_fusion.bits_ref, s32[96]{0:T(128)S(1)} %copy-done.1, bf16[96,256,256]{2,1,0:T(8,128)(2,1)} %tie_ref.7), custom_call_target="tpu_custom_call" | custom-call | tf_op jit(solution)/shard_map/partial_grams/pallas_call | solution.py:296
  15.1 2.0 %collective-permute-start.3 = (f32[2,264,128]{2,1,0:T(8,128)}, f32[2,264,128]{2,1,0:T(8,128)S(1)}, u32[]{:S(2)}, u32[]{:S(2)}) collective-permute-start(f32[2,264,128]{2,1,0:T(8,128)} %get-tuple-element.13), channel_id=1, source_target_pairs={{0,3},{1,0},{2,1},{3,2},{4,7},{5,4},{6,5},{7,6},{8,11},{9,8},{10,9... | collective-permute-start | bytes 811016 | tf_op jit(solution)/shard_map/ppermute | solution.py:344
  17.1 0.1 collective-permute-start.4
  17.2 0.0 collective-permute-done.rest_0_
  17.2 0.0 collective-permute-done.1.rest_1_
  17.2 4.6 %partial_grams.6 = (f32[2,264,128]{2,1,0:T(8,128)}, f32[2,264,128]{2,1,0:T(8,128)}) custom-call(s32[1]{0:T(128)} %bitcast.me_ref, s32[4,16]{1,0:T(4,128)S(1)} %multiply_reduce_fusion.bits_ref, s32[96]{0:T(128)S(1)} %copy-done.1, bf16[96,256,256]{2,1,0:T(8,128)(2,1)} %tie_ref.7, f32[2,264,128]{2,1,0:T(8,128)S(1)} %collective-permute-done.rest_0_, ...), custom_call_target="tpu_custom_call" | custom-call | tf_op jit(solution)/shard_map/partial_grams/pallas_call | solution.py:296
  21.8 0.8 %collective-permute-start.2 = (f32[2,264,128]{2,1,0:T(8,128)}, f32[2,264,128]{2,1,0:T(8,128)S(1)}, u32[]{:S(2)}, u32[]{:S(2)}) collective-permute-start(f32[2,264,128]{2,1,0:T(8,128)} %get-tuple-element.12), channel_id=1, source_target_pairs={{0,1},{1,2},{2,3},{3,0},{4,5},{5,6},{6,7},{7,4},{8,9},{9,10},{10,1... | collective-permute-start | bytes 811016 | tf_op jit(solution)/shard_map/ppermute | solution.py:348
  22.6 0.0 copy-start.2
  22.6 2.5 %collective-permute-start.5 = (f32[2,264,128]{2,1,0:T(8,128)}, f32[2,264,128]{2,1,0:T(8,128)S(1)}, u32[]{:S(2)}, u32[]{:S(2)}) collective-permute-start(f32[2,264,128]{2,1,0:T(8,128)} %get-tuple-element.15), channel_id=1, source_target_pairs={{0,3},{1,0},{2,1},{3,2},{4,7},{5,4},{6,5},{7,6},{8,11},{9,8},{10,9... | collective-permute-start | bytes 811016 | tf_op jit(solution)/shard_map/ppermute | solution.py:348
  25.1 4.4 %partial_grams.4.own_ref = f32[4,264,128]{2,1,0:T(8,128)S(1)} custom-call(s32[1]{0:T(128)} %bitcast.me_ref, s32[4,16]{1,0:T(4,128)S(1)} %multiply_reduce_fusion.bits_ref, s32[96]{0:T(128)S(1)} %copy-done.1, bf16[96,256,256]{2,1,0:T(8,128)(2,1)} %tie_ref.7), custom_call_target="tpu_custom_call" | custom-call | tf_op jit(solution)/shard_map/partial_grams/pallas_call | solution.py:296
  29.5 0.0 copy-done
  29.6 0.0 copy-start.3
  29.6 0.0 collective-permute-done.3.b1
  29.6 0.0 collective-permute-done.4.a0
  29.6 1.3 %collective-permute-done.2.b0 = f32[2,264,128]{2,1,0:T(8,128)S(1)} collective-permute-done((f32[2,264,128]{2,1,0:T(8,128)}, f32[2,264,128]{2,1,0:T(8,128)S(1)}, u32[]{:S(2)}, u32[]{:S(2)}) %collective-permute-start.2) | collective-permute-done | bytes 270368 | tf_op jit(solution)/shard_map/ppermute | solution.py:348
  30.9 0.0 collective-permute-done.5.a1
  30.9 0.0 copy-done.2
  30.9 9.1 %factor_scenes.1 = (f32[4,192,256]{2,1,0:T(8,128)}, f32[24,128]{1,0:T(8,128)S(1)}) custom-call(f32[4]{0:T(128)S(1)} %copy-done.2, f32[4,264,128]{2,1,0:T(8,128)S(1)} %partial_grams.4.own_ref, f32[2,264,128]{2,1,0:T(8,128)S(1)} %collective-permute-done.2.b0, f32[2,264,128]{2,1,0:T(8,128)S(1)} %collective-permute-done.3.b1, ...), custom_call_target="tpu_custom_call" | custom-call | tf_op jit(solution)/shard_map/factor_scenes/pallas_call | solution.py:166
  40.0 0.0 collective-permute-start.6
  40.0 1.2 %collective-permute-done.6 = f32[24,128]{1,0:T(8,128)S(1)} collective-permute-done((f32[24,128]{1,0:T(8,128)S(1)}, f32[24,128]{1,0:T(8,128)S(1)}, u32[]{:S(2)}, u32[]{:S(2)}) %collective-permute-start.6) | collective-permute-done | bytes 12320 | tf_op jit(solution)/shard_map/ppermute | solution.py:355
  41.2 16.4 %all_to_all.10 = f32[16,24,128]{2,1,0:T(8,128)S(1)} all-to-all(f32[16,24,128]{2,1,0:T(8,128)S(1)} %broadcast_in_dim.18), channel_id=1, replica_groups={{0,8,16,24,32,40,48,56,64,72,80,88,96,104,112,120},{4,12,20,28,36,44,52..., dimensions={0} | all-to-all | bytes 393216 | tf_op jit(solution)/shard_map/all_to_all | solution.py:327
  57.7 9.6 %all_to_all.11.parts_ref = f32[4,24,128]{2,1,0:T(8,128)S(1)} all-to-all(f32[4,24,128]{2,1,0:T(8,128)S(1)} %broadcast_in_dim.19), channel_id=1, replica_groups={{0,1,2,3},{4,5,6,7},{8,9,10,11},{12,13,14,15},{16,17,18,19},{20,21,22,2..., dimensions={0} | all-to-all | bytes 98304 | tf_op jit(solution)/shard_map/all_to_all | solution.py:327
  67.2 0.0 copy-done.3
  67.2 2.4 %factor_total.1 = f32[64,64]{1,0:T(8,128)} custom-call(f32[1,64]{1,0:T(1,128)S(1)} %bitcast.2, f32[4,24,128]{2,1,0:T(8,128)S(1)} %all_to_all.11.parts_ref), custom_call_target="tpu_custom_call" | custom-call | tf_op jit(solution)/shard_map/factor_total/pallas_call | solution.py:203
  (7 shorter events, 0.1 us)
Async XLA Ops:
  0.6 28.9 %copy-start = (bf16[16,192,192]{2,1,0:T(8,128)(2,1)S(1)}, bf16[16,192,192]{2,1,0:T(8,128)(2,1)}, u32[]{:S(2)}) copy-start(bf16[16,192,192]{2,1,0:T(8,128)(2,1)} %param.9) | copy-start | bytes 3538948
  1.6 0.7 copy-start.1
  6.7 10.5 %collective-permute-start = (f32[2,264,128]{2,1,0:T(8,128)S(1)}, f32[2,264,128]{2,1,0:T(8,128)S(1)}, u32[]{:S(2)}, u32[]{:S(2)}) collective-permute-start(f32[2,264,128]{2,1,0:T(8,128)S(1)} %get-tuple-element.10), channel_id=1, source_target_pairs={{0,1},{1,2},{2,3},{3,0},{4,5},{5,6},{6,7},{7,4},{8,9},{9,10},{10,1... | collective-permute-start | bytes 811016 | tf_op jit(solution)/shard_map/ppermute | solution.py:341
  7.9 9.3 %collective-permute-start.1 = (f32[2,264,128]{2,1,0:T(8,128)S(1)}, f32[2,264,128]{2,1,0:T(8,128)S(1)}, u32[]{:S(2)}, u32[]{:S(2)}) collective-permute-start(f32[2,264,128]{2,1,0:T(8,128)S(1)} %get-tuple-element.11), channel_id=1, source_target_pairs={{0,3},{1,0},{2,1},{3,2},{4,7},{5,4},{6,5},{7,6},{8,11},{9,8},{10,9... | collective-permute-start | bytes 811016 | tf_op jit(solution)/shard_map/ppermute | solution.py:341
  15.1 14.5 %collective-permute-start.3 = (f32[2,264,128]{2,1,0:T(8,128)}, f32[2,264,128]{2,1,0:T(8,128)S(1)}, u32[]{:S(2)}, u32[]{:S(2)}) collective-permute-start(f32[2,264,128]{2,1,0:T(8,128)} %get-tuple-element.13), channel_id=1, source_target_pairs={{0,3},{1,0},{2,1},{3,2},{4,7},{5,4},{6,5},{7,6},{8,11},{9,8},{10,9... | collective-permute-start | bytes 811016 | tf_op jit(solution)/shard_map/ppermute | solution.py:344
  17.1 12.5 %collective-permute-start.4 = (f32[2,264,128]{2,1,0:T(8,128)S(1)}, f32[2,264,128]{2,1,0:T(8,128)S(1)}, u32[]{:S(2)}, u32[]{:S(2)}) collective-permute-start(f32[2,264,128]{2,1,0:T(8,128)S(1)} %get-tuple-element.14), channel_id=1, source_target_pairs={{0,1},{1,2},{2,3},{3,0},{4,5},{5,6},{6,7},{7,4},{8,9},{9,10},{10,1... | collective-permute-start | bytes 811016 | tf_op jit(solution)/shard_map/ppermute | solution.py:344
  21.8 9.1 %collective-permute-start.2 = (f32[2,264,128]{2,1,0:T(8,128)}, f32[2,264,128]{2,1,0:T(8,128)S(1)}, u32[]{:S(2)}, u32[]{:S(2)}) collective-permute-start(f32[2,264,128]{2,1,0:T(8,128)} %get-tuple-element.12), channel_id=1, source_target_pairs={{0,1},{1,2},{2,3},{3,0},{4,5},{5,6},{6,7},{7,4},{8,9},{9,10},{10,1... | collective-permute-start | bytes 811016 | tf_op jit(solution)/shard_map/ppermute | solution.py:348
  22.6 8.2 %copy-start.2 = (f32[4]{0:T(128)S(1)}, f32[4]{0:T(128)}, u32[]{:S(2)}) copy-start(f32[4]{0:T(128)} %damp_ref.1) | copy-start | bytes 52
  22.6 8.2 %collective-permute-start.5 = (f32[2,264,128]{2,1,0:T(8,128)}, f32[2,264,128]{2,1,0:T(8,128)S(1)}, u32[]{:S(2)}, u32[]{:S(2)}) collective-permute-start(f32[2,264,128]{2,1,0:T(8,128)} %get-tuple-element.15), channel_id=1, source_target_pairs={{0,3},{1,0},{2,1},{3,2},{4,7},{5,4},{6,5},{7,6},{8,11},{9,8},{10,9... | collective-permute-start | bytes 811016 | tf_op jit(solution)/shard_map/ppermute | solution.py:348
  29.6 37.7 %copy-start.3 = (f32[64]{0:T(128)S(1)}, f32[64]{0:T(128)}, u32[]{:S(2)}) copy-start(f32[64]{0:T(128)} %param.11) | copy-start | bytes 772
  40.0 1.2 %collective-permute-start.6 = (f32[24,128]{1,0:T(8,128)S(1)}, f32[24,128]{1,0:T(8,128)S(1)}, u32[]{:S(2)}, u32[]{:S(2)}) collective-permute-start(f32[24,128]{1,0:T(8,128)S(1)} %get-tuple-element.17), channel_id=1, source_target_pairs={{0,4},{4,0},{8,12},{12,8},{16,20},{20,16},{24,28},{28,24},{32,36},... | collective-permute-start | bytes 36872 | tf_op jit(solution)/shard_map/ppermute | solution.py:355
